TPU v7x, 128 devices: a whole 4x4x4 slice. The times are simulated.
128 devices in a mesh: board: 16 (over z, x_lo, core), hand: 8 (over y, x_hi).
Axes of the slice: x: 4 (x_hi: 2, x_lo: 2; x = x_hi * 2 + x_lo), y: 4, z: 4, core: 2. Of those that a mesh axis runs over, the one named last changes fastest.
Arguments:
- cum_turn: float32 [1408, 13, 8], P(('board', 'hand')), may hold values from 0.05 to 20
- cum_river: float32 [1408, 9, 13, 384], P(('board', 'hand')), may hold values from 0.05 to 20
- opp_init: float32 [1408, 8], P(('board', 'hand')), may hold values from 0.00021306818 to 0.0021306819
- turn_cards: int32 [8, 4], replicated, may hold values from 0 to 51, as said below
- strength: int32 [1408, 384], P(('board', 'hand')), may hold values from 0 to 255, as said below
Outputs:
- river_value: float32 [384, 9, 1408], P(('board', 'hand'))
- br_value: float32 [1408, 8], P(('board', 'hand'))
Inputs may be any that keep to these rules, and one draw needn't show every extreme that they name: `turn_cards`: each row names four different cards. `strength`: on every river board some hand slot has level 0 and some has level 255.
All inputs are finite; a program needn't handle non-finite values.
Results may differ from a plain program's by a relative error of at most 0.0003.
Values may be sent and summed in bfloat16 or wider, within the bound.
No kernel may reach another device: no remote copies, remote signals or barrier semaphores. Data moves between devices by JAX's collectives and lax.ppermute only.
A program may use at most 128 MiB of HBM per device.

v0:
```python
import jax
import jax.numpy as jnp
import numpy as np
from jax import lax
from jax.sharding import PartitionSpec as P

LIVE = 1326
RIVERS = 48
BETS = 4


pre_pot = 2.0


def grow_street(bet_cap):
    tree_nodes = []

    def add_leaf(leaf_kind, folder, put_zero, put_one):
        tree_nodes.append(
            {
                "kind": leaf_kind,
                "player": -1,
                "folder": folder,
                "put": (put_zero, put_one),
                "children": [],
            }
        )
        return len(tree_nodes) - 1

    def grow_node(player, bet_count, put_zero, put_one):
        position = len(tree_nodes)
        tree_nodes.append(
            {
                "kind": "act",
                "player": player,
                "folder": -1,
                "put": (put_zero, put_one),
                "children": [],
            }
        )
        own_put = put_zero if player == 0 else put_one
        rival_put = put_one if player == 0 else put_zero
        raised = rival_put + 1
        after_zero = raised if player == 0 else put_zero
        after_one = raised if player == 1 else put_one
        children = []
        if rival_put > own_put:
            children.append(add_leaf("fold", player, put_zero, put_one))
            children.append(add_leaf("end", -1, rival_put, rival_put))
        elif player == 0:
            children.append(grow_node(1, bet_count, put_zero, put_one))
        else:
            children.append(add_leaf("end", -1, put_zero, put_one))
        if bet_count < bet_cap:
            children.append(grow_node(1 - player, bet_count + 1, after_zero, after_one))
        tree_nodes[position]["children"] = children
        return position

    grow_node(0, 0, 0, 0)
    return tree_nodes


def street_tables(bet_cap):
    tree_nodes = grow_street(bet_cap)
    end_leaves = [
        node_id for node_id in range(len(tree_nodes)) if tree_nodes[node_id]["kind"] == "end"
    ]
    fold_leaves = [
        node_id for node_id in range(len(tree_nodes)) if tree_nodes[node_id]["kind"] == "fold"
    ]
    row_of = {}
    for node_id in range(len(tree_nodes)):
        if tree_nodes[node_id]["kind"] == "act" and tree_nodes[node_id]["player"] == 1:
            for child_id in tree_nodes[node_id]["children"]:
                row_of[child_id] = len(row_of)
    return (tree_nodes, end_leaves, fold_leaves, row_of)


def leaf_scales(tree_nodes, end_leaves, fold_leaves, line_puts):
    end_scale = np.zeros((len(line_puts), len(end_leaves)), np.float32)
    fold_scale = np.zeros((len(line_puts), len(fold_leaves)), np.float32)
    for line_id in range(len(line_puts)):
        for column, leaf_id in enumerate(end_leaves):
            end_scale[line_id, column] = (
                pre_pot + line_puts[line_id][0] + tree_nodes[leaf_id]["put"][0]
            )
        for column, leaf_id in enumerate(fold_leaves):
            folder = tree_nodes[leaf_id]["folder"]
            loser_put = pre_pot + line_puts[line_id][folder] + tree_nodes[leaf_id]["put"][folder]
            fold_scale[line_id, column] = loser_put if folder == 1 else -loser_put
    return (end_scale, fold_scale)


def hand_cards(hand_count):
    card_low = []
    card_high = []
    for low_card in range(52):
        for high_card in range(low_card + 1, 52):
            card_low.append(low_card)
            card_high.append(high_card)
    card_low = (card_low + [52] * hand_count)[:hand_count]
    card_high = (card_high + [53] * hand_count)[:hand_count]
    return (np.array(card_low, np.int32), np.array(card_high, np.int32))


def make_shares(tree_nodes, row_of, picker):
    shares = {}
    for node_id in range(len(tree_nodes)):
        if tree_nodes[node_id]["kind"] == "act" and tree_nodes[node_id]["player"] == 1:
            children = tree_nodes[node_id]["children"]
            summed = picker(row_of[children[0]])
            for child_id in children[1:]:
                summed = summed + picker(row_of[child_id])
            for child_id in children:
                shares[child_id] = picker(row_of[child_id]) / summed
    return shares


def spread_reach(tree_nodes, shares, root_reach):
    reach_map = {0: root_reach}
    for node_id in range(len(tree_nodes)):
        if tree_nodes[node_id]["kind"] != "act":
            continue
        for child_id in tree_nodes[node_id]["children"]:
            if tree_nodes[node_id]["player"] == 1:
                reach_map[child_id] = reach_map[node_id] * shares[child_id]
            else:
                reach_map[child_id] = reach_map[node_id]
    return reach_map


def back_up(tree_nodes, leaf_values):
    values = dict(leaf_values)
    for node_id in reversed(range(len(tree_nodes))):
        if tree_nodes[node_id]["kind"] != "act":
            continue
        child_values = [values[child_id] for child_id in tree_nodes[node_id]["children"]]
        merged = child_values[0]
        for other_value in child_values[1:]:
            if tree_nodes[node_id]["player"] == 0:
                merged = jnp.maximum(merged, other_value)
            else:
                merged = merged + other_value
        values[node_id] = merged
    return values[0]


def board_values(hand_level, leaf_reach, apart_pairs, tree_parts):
    tree_nodes, end_leaves, fold_leaves, end_scale, fold_scale = tree_parts
    line_count = leaf_reach.shape[0]
    hand_count = leaf_reach.shape[2]
    ends_count = len(end_leaves)
    level_float = hand_level.astype(jnp.float32)
    living = level_float >= 0.0
    allowed = apart_pairs & living[:, None] & living[None, :]
    end_rows = leaf_reach[:, :ends_count, :].reshape(-1, hand_count)
    fold_rows = leaf_reach[:, ends_count:, :].reshape(-1, hand_count)
    contract = (((1,), (1,)), ((), ()))
    sign_matrix = jnp.where(
        allowed, jnp.sign(level_float[:, None] - level_float[None, :]), 0.0
    ).astype(jnp.bfloat16)
    showdown_sums = lax.dot_general(
        end_rows, sign_matrix, contract, preferred_element_type=jnp.float32
    ).reshape(line_count, ends_count, hand_count)
    pair_mask = allowed.astype(jnp.bfloat16)
    fold_sums = lax.dot_general(fold_rows, pair_mask, contract, preferred_element_type=jnp.float32)
    fold_sums = fold_sums.reshape(line_count, -1, hand_count)
    leaf_values = {}
    for column, leaf_id in enumerate(end_leaves):
        leaf_values[leaf_id] = showdown_sums[:, column, :] * end_scale[:, column][:, None]
    for column, leaf_id in enumerate(fold_leaves):
        leaf_values[leaf_id] = fold_sums[:, column, :] * fold_scale[:, column][:, None]
    return back_up(tree_nodes, leaf_values)


def to_owners(packed, device_count, local_boards):
    owned, row_width, board_count = packed.shape
    packed = packed.reshape(owned, row_width, device_count, local_boards)
    return jnp.transpose(packed, (2, 3, 0, 1)).reshape(
        device_count, local_boards, owned * row_width
    )


def from_owners(packed, row_width):
    item_count = packed.shape[1]
    packed = packed.reshape(item_count, -1, row_width)
    return jnp.transpose(packed, (0, 2, 1))


def body(cum_turn, cum_river, opp_init, turn_cards, strength):
    device_count = lax.axis_size(("board", "hand"))
    my_index = lax.axis_index(("board", "hand"))
    owned = cum_river.shape[0]
    line_count = cum_river.shape[1]
    row_count = cum_river.shape[2]
    board_count = cum_river.shape[3]
    turn_count = cum_turn.shape[2]
    hand_count = owned * device_count
    local_boards = board_count // device_count
    tree_nodes, end_leaves, fold_leaves, row_of = street_tables(BETS)
    line_puts = [tree_nodes[leaf_id]["put"] for leaf_id in end_leaves]
    end_scale, fold_scale = leaf_scales(tree_nodes, end_leaves, fold_leaves, line_puts)
    unused_scale, turn_fold_scale = leaf_scales(tree_nodes, end_leaves, fold_leaves, [(0, 0)])
    tree_parts = (tree_nodes, end_leaves, fold_leaves, end_scale, fold_scale)
    low_table, high_table = hand_cards(hand_count)
    full_low = jnp.asarray(low_table)
    full_high = jnp.asarray(high_table)
    deck_cards = jnp.arange(52, dtype=jnp.int32)
    offset = my_index * owned
    card_low = lax.dynamic_slice_in_dim(full_low, offset, owned)
    card_high = lax.dynamic_slice_in_dim(full_high, offset, owned)
    hand_ids = offset + jnp.arange(owned, dtype=jnp.int32)
    in_turn = jnp.any(turn_cards[:, :, None] == deck_cards[None, None, :], axis=1)
    rest_rank = jnp.cumsum(jnp.where(in_turn, 0, 1).astype(jnp.int32), axis=1, dtype=jnp.int32) - 1
    picked = (
        rest_rank[:, None, :] == jnp.arange(RIVERS, dtype=jnp.int32)[None, :, None]
    ) & jnp.logical_not(in_turn)[:, None, :]
    river_card = jnp.sum(
        jnp.where(picked, deck_cards[None, None, :], 0), axis=2, dtype=jnp.int32
    ).reshape(board_count)
    blocked = jnp.any(
        (card_low[:, None, None] == turn_cards[None, :, :])
        | (card_high[:, None, None] == turn_cards[None, :, :]),
        axis=2,
    )
    alive_turn = (hand_ids < LIVE)[:, None] & jnp.logical_not(blocked)
    alive_river = (
        jnp.repeat(alive_turn, RIVERS, axis=1)
        & (card_low[:, None] != river_card[None, :])
        & (card_high[:, None] != river_card[None, :])
    )
    card_marks = (
        (card_low[:, None] == deck_cards[None, :]) | (card_high[:, None] == deck_cards[None, :])
    ).astype(jnp.float32)
    turn_shares = make_shares(tree_nodes, row_of, lambda row_id: cum_turn[:, row_id, :])
    turn_reach = spread_reach(tree_nodes, turn_shares, opp_init * alive_turn.astype(jnp.float32))
    line_reach = jnp.stack([turn_reach[leaf_id] for leaf_id in end_leaves], axis=1)
    fold_reach = jnp.stack([turn_reach[leaf_id] for leaf_id in fold_leaves], axis=1)
    card_sums = jnp.einsum("hc,hft->cft", card_marks, fold_reach, precision=lax.Precision.HIGHEST)
    fold_totals = jnp.sum(fold_reach, axis=0)
    card_sums, fold_totals = lax.psum((card_sums, fold_totals), ("board", "hand"))
    root_reach = jnp.repeat(line_reach, RIVERS, axis=2) * alive_river[:, None, :].astype(
        jnp.float32
    )
    hand_level = jnp.where(alive_river, strength, -1).astype(jnp.float32)[:, None, :]
    apart_pairs = (
        (full_low[:, None] != full_low[None, :])
        & (full_low[:, None] != full_high[None, :])
        & (full_high[:, None] != full_low[None, :])
        & (full_high[:, None] != full_high[None, :])
    )

    def evaluate(levels_in, leaf_reach):

        def one_board(pieces):
            return board_values(pieces[0], pieces[1], apart_pairs, tree_parts)

        return lax.map(one_board, (levels_in, leaf_reach))

    rows_out = to_owners(
        cum_river.reshape(owned, line_count * row_count, board_count), device_count, local_boards
    )
    root_out = to_owners(root_reach, device_count, local_boards)
    levels_out = to_owners(hand_level, device_count, local_boards)

    def settle_rows(pieces):
        cum_in = from_owners(pieces[0], line_count * row_count)
        item_count = cum_in.shape[0]
        cum_in = cum_in.reshape(item_count, line_count, row_count, hand_count)
        root_in = from_owners(pieces[1], line_count)
        levels_in = from_owners(pieces[2], 1)[:, 0, :]
        shares = make_shares(tree_nodes, row_of, lambda row_id: cum_in[:, :, row_id, :])
        reach_map = spread_reach(tree_nodes, shares, root_in)
        leaf_reach = jnp.stack(
            [reach_map[leaf_id] for leaf_id in end_leaves + fold_leaves], axis=2
        ).astype(jnp.bfloat16)
        return evaluate(levels_in, leaf_reach)

    river_value = settle_rows(
        (
            lax.all_to_all(rows_out, ("board", "hand"), split_axis=0, concat_axis=2, tiled=True),
            lax.all_to_all(root_out, ("board", "hand"), split_axis=0, concat_axis=2, tiled=True),
            lax.all_to_all(levels_out, ("board", "hand"), split_axis=0, concat_axis=2, tiled=True),
        )
    )
    board_ids = my_index * local_boards + jnp.arange(local_boards, dtype=jnp.int32)
    member = (
        board_ids[:, None] // RIVERS == jnp.arange(turn_count, dtype=jnp.int32)[None, :]
    ).astype(jnp.float32)
    partial_value = jnp.einsum("kt,klh->tlh", member, river_value, precision=lax.Precision.HIGHEST)
    summed_all = lax.psum(partial_value, ("board", "hand"))
    owned_share = lax.dynamic_slice_in_dim(summed_all, offset, owned, 2)
    line_values = jnp.transpose(owned_share, (2, 1, 0)) / RIVERS
    looked = jnp.einsum("hc,cft->hft", card_marks, card_sums, precision=lax.Precision.HIGHEST)
    fold_sums = alive_turn.astype(jnp.float32)[:, None, :] * (
        fold_totals[None, :, :] - looked + fold_reach
    )
    leaf_values = {}
    for column, leaf_id in enumerate(end_leaves):
        leaf_values[leaf_id] = line_values[:, column, :]
    for column, leaf_id in enumerate(fold_leaves):
        leaf_values[leaf_id] = fold_sums[:, column, :] * turn_fold_scale[0, column]
    br_value = back_up(tree_nodes, leaf_values)
    return (river_value, br_value)


def solution(mesh):
    placed = (
        P(("board", "hand"), None, None),
        P(("board", "hand"), None, None, None),
        P(("board", "hand"), None),
        P(),
        P(("board", "hand"), None),
    )
    return jax.shard_map(
        body,
        mesh=mesh,
        in_specs=placed,
        out_specs=(P(("board", "hand"), None, None), P(("board", "hand"), None)),
        check_vma=False,
    )
```

profile of v0, /device:TPU:1, one launch (start us, length us, event | category | flops | bytes accessed | tf_op | source)
XLA Modules:
  0.0 484.9 jit_solution(7063789828400684932)
XLA Ops:
  13.4 11.5 %all-to-all-start.2 = ((f32[128,3,11]{2,1,0:T(4,128)}), f32[128,3,11]{2,1,0:T(4,128)S(1)}, u32[]{:S(2)}, u32[]{:S(2)}) async-start(f32[128,3,11]{2,1,0:T(4,128)} %bitcast.61), calls=%async_computation.2 | async-start | bytes 524288 | tf_op jit(solution)/shard_map/all_to_all | solution.py:283
  25.3 1.8 fusion.130
  30.5 5.7 %all-to-all-done.2 = f32[128,3,11]{2,1,0:T(4,128)S(1)} async-done(((f32[128,3,11]{2,1,0:T(4,128)}), f32[128,3,11]{2,1,0:T(4,128)S(1)}, u32[]{:S(2)}, u32[]{:S(2)}) %all-to-all-start.2) | async-done | bytes 16928 | tf_op jit(solution)/shard_map/all_to_all | solution.py:283
  36.2 4.9 %all-to-all-start = ((f32[128,3,99]{2,1,0:T(4,128)}), f32[128,3,99]{2,1,0:T(4,128)}, u32[]{:S(2)}, u32[]{:S(2)}) async-start(f32[128,3,99]{2,1,0:T(4,128)} %copy.285), calls=%async_computation | async-start | bytes 524288 | tf_op jit(solution)/shard_map/all_to_all | solution.py:282
  41.1 19.8 %copy.287 = f32[11,9,13,384]{2,1,3,0:T(8,128)} copy(f32[11,9,13,384]{3,2,1,0:T(8,128)S(1)} %copy-done.4) | data formatting | bytes 3953664 | tf_op args[1]
  60.9 22.8 %reshape_reshape.3 = f32[11,117,128,3]{1,3,2,0:T(4,128)} reshape(f32[11,9,13,384]{2,1,3,0:T(8,128)} %copy.287) | data formatting | bytes 3953664 | tf_op jit(solution)/shard_map/reshape;reshape | solution.py:178
  83.7 3.1 copy.327
  86.8 4.0 reshape.912
  90.8 9.9 %all-to-all-start.1 = ((f32[128,3,1287]{2,1,0:T(4,128)}), f32[128,3,1287]{2,1,0:T(4,128)S(1)}, u32[]{:S(2)}, u32[]{:S(2)}) async-start(f32[128,3,1287]{2,1,0:T(4,128)} %reshape.912), calls=%async_computation.1 | async-start | bytes 5767168 | tf_op jit(solution)/shard_map/all_to_all | solution.py:281
  101.1 90.6 %all-reduce = (f32[52,8,8]{0,2,1:T(8,128)}, f32[8,8]{1,0:T(8,128)}) all-reduce(f32[52,8,8]{0,2,1:T(8,128)S(1)} %convolution_bitcast_fusion.1, f32[8,8]{1,0:T(8,128)S(1)} %reduce_sum.19), channel_id=1, replica_groups=mesh['board'=16,'hand'=8] {'board','hand'}, use_global_device_ids=true, to_apply=%region_9.10 | all-reduce | flops 3392 | bytes 27136 | tf_op jit(solution)/shard_map/psum | solution.py:241
  193.1 1.0 copy.286
  194.0 2.0 reshape.891
  196.0 1.5 copy.290
  197.5 2.6 reshape.893
  200.1 2.1 copy.291
  202.2 1.6 reshape.894
  203.9 2.2 fusion.129
  206.1 2.7 copy.353
  208.8 1.8 copy.354
  210.6 1.8 copy.352
  212.5 1.9 copy.349
  214.3 1.8 copy.350
  216.2 1.8 copy.351
  218.0 1.8 copy.343
  219.8 1.8 copy.342
  221.7 1.1 copy.347
  222.8 1.8 copy.348
  224.6 1.9 copy.344
  226.5 1.8 copy.345
  228.3 1.8 copy.346
  230.2 14.8 %fusion.77 = (bf16[3,9,1,1408]{1,3,0,2:T(8,128)(2,1)}, f32[3,9,1408]{1,2,0:T(8,128)}, bf16[3,9,1,1408]{1,3,0,2:T(8,128)(2,1)}, bf16[3,9,1,1408]{1,3,0,2:T(8,128)...) fusion(f32[3,9,1,1408]{1,3,0,2:T(8,128)} %copy.353, ...), kind=kLoop, calls=%fused_computation.120 | loop fusion | flops 1102464 | bytes 2965248 | tf_op jit(solution)/shard_map/stack | solution.py:274
  246.2 8.9 %fusion.73 = (bf16[3,9,1,1408]{1,3,0,2:T(8,128)(2,1)S(1)}, bf16[3,9,1,1408]{1,3,0,2:T(8,128)(2,1)}, bf16[3,9,1,1408]{1,3,0,2:T(8,128)(2,1)}, bf16[3,9,1,1408]{1,3,0,2:T(8,128)(2,1)}, bf16[3,9,1,1408]{1,3,0,2:T(8,128)(2,1)}) fusion(f32[3,9,1408]{1,2,0:T(8,128)} %get-tuple-element.302, f32[3,9,1,1408]{1,3,0,2:T(8,128)} %copy.345, ...), kind=kLoop, calls=%fused_computation.116 | loop fusion | flops 532224 | bytes 1444608 | tf_op jit(solution)/shard_map/stack | solution.py:274
  255.2 2.4 copy.307
  257.5 2.5 copy.308
  260.0 1.7 copy.309
  261.8 2.4 copy.310
  264.2 2.4 copy.311
  266.5 5.8 %fusion.54 = (bf16[3,9,1408]{1,2,0:T(8,128)(2,1)}, bf16[3,9,1,1408]{1,3,0,2:T(8,128)(2,1)}, bf16[3,9,1,1408]{1,3,0,2:T(8,128)(2,1)}) fusion(f32[3,9,1408]{1,2,0:T(8,128)} %get-tuple-element.275, f32[3,9,1,1408]{1,3,0,2:T(8,128)} %copy.354, f32[3,9,1,1408]{1,3,0,2:T(8,128)} %copy.352, f32[3,9,1,1408]{1,3,0,2:T(8,128)S(1)} %copy-done), kind=kLoop, calls=%fused_computation.79 | loop fusion | flops 342144 | bytes 836352 | tf_op jit(solution)/shard_map/convert.8
  272.4 1.8 copy.312
  274.2 2.4 copy.313
  277.8 1.7 constant_dynamic-update-slice_fusion.21
  280.2 1.6 constant_dynamic-update-slice_fusion.19
  281.7 1.6 constant_dynamic-update-slice_fusion.18
  284.0 1.6 constant_dynamic-update-slice_fusion.16
  286.3 1.6 constant_dynamic-update-slice_fusion.15
  287.9 1.1 copy.316
  289.0 1.6 constant_dynamic-update-slice_fusion.14
  291.3 1.7 copy.318
  297.7 1.7 copy.326
  299.6 34.4 %while.13 = (s32[]{:T(128)}, f32[3,9,1408]{2,0,1:T(4,128)S(1)}, bf16[3,9,17,1408]{3,2,1,0:T(8,128)(2,1)S(1)}, f32[3,1408]{1,0:T(4,128)S(1)}, s32[1408]{0:T(1024)...) while((s32[]{:T(128)}, f32[3,9,1408]{2,0,1:T(4,128)S(1)}, ...), condition=%wide.region_5.6_spmd.clone.clone.clone, body=%wide.region_4.5_spmd.sunk.clone.clone.clone.sunk | while | flops 650669184 | bytes 3461369 | solution.py:258
  300.0 5.4 %fusion.143 = f32[9,9,1408]{2,1,0:T(8,128)S(1)} fusion(f32[1408]{0:T(1024)S(1)} %dynamic-slice_reduce_fusion.2, s32[1408]{0:T(1024)S(1)} %get-tuple-element.408, s32[1408]{0:T(1024)S(1)} %get-tuple-element.407, pred[1408]{0:T(1024)(128)(4,1)S(1)} %broadcast_compare_fusion.2, pred[1408]{0:T(1024)(128)(4,1)S(1)} %compare_reduce_fusion.2, ...), kind=kOutput, calls=%fused_computation.7.clone.1 | convolution fusion | flops 346931200 | bytes 914944 | tf_op jit(solution)/shard_map/while/body/eval_jaxpr/dot_general | solution.py:162
  305.4 3.6 fusion.144
  309.0 0.9 fusion.145
  309.9 1.3 dynamic_update_slice.9
  311.4 5.4 %fusion.143 = f32[9,9,1408]{2,1,0:T(8,128)S(1)} fusion(f32[1408]{0:T(1024)S(1)} %dynamic-slice_reduce_fusion.2, s32[1408]{0:T(1024)S(1)} %get-tuple-element.408, s32[1408]{0:T(1024)S(1)} %get-tuple-element.407, pred[1408]{0:T(1024)(128)(4,1)S(1)} %broadcast_compare_fusion.2, pred[1408]{0:T(1024)(128)(4,1)S(1)} %compare_reduce_fusion.2, ...), kind=kOutput, calls=%fused_computation.7.clone.1 | convolution fusion | flops 346931200 | bytes 914944 | tf_op jit(solution)/shard_map/while/body/eval_jaxpr/dot_general | solution.py:162
  316.8 3.6 fusion.144
  320.4 0.9 fusion.145
  321.3 1.3 dynamic_update_slice.9
  322.8 5.4 %fusion.143 = f32[9,9,1408]{2,1,0:T(8,128)S(1)} fusion(f32[1408]{0:T(1024)S(1)} %dynamic-slice_reduce_fusion.2, s32[1408]{0:T(1024)S(1)} %get-tuple-element.408, s32[1408]{0:T(1024)S(1)} %get-tuple-element.407, pred[1408]{0:T(1024)(128)(4,1)S(1)} %broadcast_compare_fusion.2, pred[1408]{0:T(1024)(128)(4,1)S(1)} %compare_reduce_fusion.2, ...), kind=kOutput, calls=%fused_computation.7.clone.1 | convolution fusion | flops 346931200 | bytes 914944 | tf_op jit(solution)/shard_map/while/body/eval_jaxpr/dot_general | solution.py:162
  328.2 3.6 fusion.144
  332.7 1.3 dynamic_update_slice.9
  334.0 1.2 fusion.118
  335.5 140.5 %all-reduce.3.cloned.1.call-done = f32[8,9,1408]{2,0,1:T(8,128)} async-done(((f32[8,9,1408]{2,0,1:T(8,128)}), f32[8,9,1408]{2,0,1:T(8,128)}) %all-reduce.3.cloned.1.call-update) | async-done | bytes 405520 | tf_op jit(solution)/shard_map/psum | solution.py:291
  476.0 1.0 multiply_bitcast_fusion
  (161 shorter events, 23.5 us)
Async XLA Ops:
  7.2 21.8 %copy-start.16 = (f32[11,8]{0,1:T(8,128)S(1)}, f32[11,8]{0,1:T(8,128)}, u32[]{:S(2)}) copy-start(f32[11,8]{0,1:T(8,128)} %param.28) | copy-start | bytes 1060
  9.7 91.1 %copy-start.26 = (s32[11]{0:T(128)}, s32[11]{0:T(128)S(1)}, u32[]{:S(2)}) copy-start(s32[11]{0:T(128)S(1)} %dynamic_slice.17) | copy-start | bytes 136
  13.4 22.8 %all-to-all-start.2 = ((f32[128,3,11]{2,1,0:T(4,128)}), f32[128,3,11]{2,1,0:T(4,128)S(1)}, u32[]{:S(2)}, u32[]{:S(2)}) async-start(f32[128,3,11]{2,1,0:T(4,128)} %bitcast.61), calls=%async_computation.2 | async-start | bytes 524288 | tf_op jit(solution)/shard_map/all_to_all | solution.py:283
  25.3 15.8 %copy-start.4 = (f32[11,9,13,384]{3,2,1,0:T(8,128)S(1)}, f32[11,9,13,384]{3,2,1,0:T(8,128)}, u32[]{:S(2)}) copy-start(f32[11,9,13,384]{3,2,1,0:T(8,128)} %param.27) | copy-start | bytes 5930500
  29.1 71.8 %copy-start.14 = (f32[11,8,8]{0,2,1:T(8,128)}, f32[11,8,8]{0,2,1:T(8,128)S(1)}, u32[]{:S(2)}) copy-start(f32[11,8,8]{0,2,1:T(8,128)S(1)} %get-tuple-element.266) | copy-start | bytes 8452
  36.2 54.6 %all-to-all-start = ((f32[128,3,99]{2,1,0:T(4,128)}), f32[128,3,99]{2,1,0:T(4,128)}, u32[]{:S(2)}, u32[]{:S(2)}) async-start(f32[128,3,99]{2,1,0:T(4,128)} %copy.285), calls=%async_computation | async-start | bytes 524288 | tf_op jit(solution)/shard_map/all_to_all | solution.py:282
  90.8 105.2 %all-to-all-start.1 = ((f32[128,3,1287]{2,1,0:T(4,128)}), f32[128,3,1287]{2,1,0:T(4,128)S(1)}, u32[]{:S(2)}, u32[]{:S(2)}) async-start(f32[128,3,1287]{2,1,0:T(4,128)} %reshape.912), calls=%async_computation.1 | async-start | bytes 5767168 | tf_op jit(solution)/shard_map/all_to_all | solution.py:281
  100.7 375.3 %all-reduce.3.cloned.1.call-start = ((), (), s32[]{:S(2)}) async-start(), calls=%async_computation.3 | async-start | bytes 811008 | tf_op jit(solution)/shard_map/psum | solution.py:291
  206.0 2.7 copy-start.10
  206.0 4.5 copy-start.9
  208.8 3.7 copy-start.8
  210.6 3.7 copy-start.7
  212.4 3.7 copy-start.6
  257.5 9.0 %copy-start = (f32[3,9,1,1408]{1,3,0,2:T(8,128)S(1)}, f32[3,9,1,1408]{1,3,0,2:T(8,128)}, u32[]{:S(2)}) copy-start(f32[3,9,1,1408]{1,3,0,2:T(8,128)} %copy.353) | copy-start | bytes 456196
  272.4 4.2 copy-start.1
  272.4 4.7 copy-start.5
  277.8 15.2 %copy-start.3 = (bf16[3,9,1,1408]{1,3,0,2:T(8,128)(2,1)S(1)}, bf16[3,9,1,1408]{1,3,0,2:T(8,128)(2,1)}, u32[]{:S(2)}) copy-start(bf16[3,9,1,1408]{1,3,0,2:T(8,128)(2,1)} %get-tuple-element.279) | copy-start | bytes 228100
  287.9 7.7 %copy-start.2 = (bf16[3,9,1,1408]{1,3,0,2:T(8,128)(2,1)S(1)}, bf16[3,9,1,1408]{1,3,0,2:T(8,128)(2,1)}, u32[]{:S(2)}) copy-start(bf16[3,9,1,1408]{1,3,0,2:T(8,128)(2,1)} %get-tuple-element.274) | copy-start | bytes 228100
  296.1 3.2 copy-start.11
  296.1 3.2 copy-start.12
  296.2 3.2 copy-start.17
  296.2 3.2 copy-start.18
  296.2 3.2 copy-start.19
  296.2 3.2 copy-start.20
  296.2 3.2 copy-start.21
  296.2 3.2 copy-start.22
  296.2 3.2 copy-start.23
  296.2 3.2 copy-start.24
  296.3 3.2 copy-start.25
  296.3 3.2 copy-start.32
  296.3 3.2 copy-start.33
  299.5 34.5 %copy-start.29 = (s32[3]{0:T(128)S(1)}, s32[3]{0:T(128)}, u32[]{:S(2)}) copy-start(s32[3]{0:T(128)} %and_select_fusion) | copy-start | bytes 40
  299.5 35.8 %copy-start.15 = (f32[11,8,8]{0,2,1:T(8,128)S(1)}, f32[11,8,8]{0,2,1:T(8,128)}, u32[]{:S(2)}) copy-start(f32[11,8,8]{0,2,1:T(8,128)} %copy-done.14) | copy-start | bytes 8452
  299.5 35.8 %copy-start.27 = (s32[11]{0:T(128)S(1)}, s32[11]{0:T(128)}, u32[]{:S(2)}) copy-start(s32[11]{0:T(128)} %copy-done.26) | copy-start | bytes 136
  299.5 35.8 %copy-start.28 = (f32[11,8]{0,1:T(8,128)S(1)}, f32[11,8]{0,1:T(8,128)}, u32[]{:S(2)}) copy-start(f32[11,8]{0,1:T(8,128)} %get-tuple-element.264) | copy-start | bytes 1060
  299.5 35.8 %copy-start.30 = (f32[52,8,8]{0,2,1:T(8,128)S(1)}, f32[52,8,8]{0,2,1:T(8,128)}, u32[]{:S(2)}) copy-start(f32[52,8,8]{0,2,1:T(8,128)} %get-tuple-element.262) | copy-start | bytes 39940
  299.5 35.8 %copy-start.31 = (f32[8,8]{1,0:T(8,128)S(1)}, f32[8,8]{1,0:T(8,128)}, u32[]{:S(2)}) copy-start(f32[8,8]{1,0:T(8,128)} %get-tuple-element.263) | copy-start | bytes 772
  334.0 143.6 %copy-start.13 = (f32[3,9,1408]{2,0,1:T(4,128)}, f32[3,9,1408]{2,0,1:T(4,128)S(1)}, u32[]{:S(2)}) copy-start(f32[3,9,1408]{2,0,1:T(4,128)S(1)} %get-tuple-element.112) | copy-start | bytes 456196
Sparse Core Ops, SparseCore 0:
  335.4 140.5 all-reduce.2
where the time goes:
time: 492 us; the launch traced here: 485 us
  waiting for transfers between devices  146 us (30%)
  local copies, waits for them, and re-layouts  139 us (28%)
  blocking collectives  90.6 us (18%)
  other arithmetic  38.3 us (8%)
  matrix products  28.7 us (6%)
  starting transfers between devices  26.3 us (5%)
  between operations  15.1 us (3%)
    psum x1, waiting for transfers between devices, body(): summed_all = lax.psum(partial_value, ('board', 'hand'))  140 us
    psum x1, blocking collectives, body(): lax.psum((card_sums, fold_totals), ('board', 'hand'))  90.6 us
    unnamed x113, local copies, waits for them, and re-layouts  64 us
    another operation x2, other arithmetic, settle_rows(): jnp.stack([reach_map[leaf_id] for leaf_id in end_leaves + fold_leaves], a...  23.8 us
    another operation x2, local copies, waits for them, and re-layouts, to_owners(): packed = packed.reshape(owned, row_width, device_count, local_boards)  23.6 us
    dot_general x3, matrix products, board_values(): lax.dot_general(end_rows, sign_matrix, contract, preferred_element_type=j...  16.2 us
    another operation x10, local copies, waits for them, and re-layouts, settle_rows(): jnp.stack([reach_map[leaf_id] for leaf_id in end_leaves + fold_leaves], a...  14.8 us
    all_to_all x1, starting transfers between devices, body(): lax.all_to_all(levels_out, ('board', 'hand'), split_axis=0, concat_axis=2...  11.5 us
  transfers between devices with their start and end apart: 4, of which 2 were waited for; matrix products, arithmetic and copies ran while one was open for 12% of the time, Pallas kernels for 0%

commit v1 on v0

v1 whole, which is shorter than its diff:
```python
import jax
import jax.numpy as jnp
import numpy as np
from jax import lax
from jax.experimental import pallas as pl
from jax.experimental.pallas import tpu as pltpu
from jax.sharding import PartitionSpec as P

LIVE = 1326
RIVERS = 48
BETS = 4
PRE_POT = 2.0
AXES = ("board", "hand")

HANDS = 1408
DEVICES = 128
OWNED = HANDS // DEVICES
LINES = 9
ROWS = 13
BOARDS = 384
TURNS = 8
LOCAL = BOARDS // DEVICES
SLOTS = 120
BOARD_SLOTS = OWNED * SLOTS
BLOCKS = 32
USED_BLOCKS = 31
LEVEL_SLOT = 117
VMEM = 56 * 1024 * 1024


def grow_street(bet_cap):
    tree_nodes = []

    def add_leaf(leaf_kind, folder, put_zero, put_one):
        tree_nodes.append(
            {
                "kind": leaf_kind,
                "player": -1,
                "folder": folder,
                "put": (put_zero, put_one),
                "children": [],
            }
        )
        return len(tree_nodes) - 1

    def grow_node(player, bet_count, put_zero, put_one):
        position = len(tree_nodes)
        tree_nodes.append(
            {
                "kind": "act",
                "player": player,
                "folder": -1,
                "put": (put_zero, put_one),
                "children": [],
            }
        )
        own_put = put_zero if player == 0 else put_one
        rival_put = put_one if player == 0 else put_zero
        raised = rival_put + 1
        after_zero = raised if player == 0 else put_zero
        after_one = raised if player == 1 else put_one
        children = []
        if rival_put > own_put:
            children.append(add_leaf("fold", player, put_zero, put_one))
            children.append(add_leaf("end", -1, rival_put, rival_put))
        elif player == 0:
            children.append(grow_node(1, bet_count, put_zero, put_one))
        else:
            children.append(add_leaf("end", -1, put_zero, put_one))
        if bet_count < bet_cap:
            children.append(grow_node(1 - player, bet_count + 1, after_zero, after_one))
        tree_nodes[position]["children"] = children
        return position

    grow_node(0, 0, 0, 0)
    return tree_nodes


TREE = grow_street(BETS)
ENDS = [i for i, node in enumerate(TREE) if node["kind"] == "end"]
FOLDS = [i for i, node in enumerate(TREE) if node["kind"] == "fold"]
ROW_OF = {}
for _i, _node in enumerate(TREE):
    if _node["kind"] == "act" and _node["player"] == 1:
        for _child in _node["children"]:
            ROW_OF[_child] = len(ROW_OF)
REACH_ROW = dict(ROW_OF)
for _i, _node in enumerate(TREE):
    if _node["kind"] == "act" and _node["player"] == 0 and _i > 0:
        for _child in _node["children"]:
            REACH_ROW[_child] = REACH_ROW[_i]
LINE_PUT = [TREE[i]["put"][0] for i in ENDS]


def hand_cards(hand_count):
    card_low = []
    card_high = []
    for low_card in range(52):
        for high_card in range(low_card + 1, 52):
            card_low.append(low_card)
            card_high.append(high_card)
    card_low = (card_low + [52] * hand_count)[:hand_count]
    card_high = (card_high + [53] * hand_count)[:hand_count]
    return np.array(card_low, np.int32), np.array(card_high, np.int32)


def back_up(leaf_values):
    values = dict(leaf_values)
    for node_id in reversed(range(len(TREE))):
        if TREE[node_id]["kind"] != "act":
            continue
        child_values = [values[child_id] for child_id in TREE[node_id]["children"]]
        merged = child_values[0]
        for other_value in child_values[1:]:
            if TREE[node_id]["player"] == 0:
                merged = jnp.maximum(merged, other_value)
            else:
                merged = merged + other_value
        values[node_id] = merged
    return values[0]


def node_rows():
    nodes = []
    for i, node in enumerate(TREE):
        if node["kind"] == "act" and node["player"] == 1:
            parent = REACH_ROW.get(i, -1)
            nodes.append((parent, [ROW_OF[c] for c in node["children"]]))
    return nodes


def sort_four(cards):
    a, b, c, d = cards
    a, b = jnp.minimum(a, b), jnp.maximum(a, b)
    c, d = jnp.minimum(c, d), jnp.maximum(c, d)
    a, c = jnp.minimum(a, c), jnp.maximum(a, c)
    b, d = jnp.minimum(b, d), jnp.maximum(b, d)
    b, c = jnp.minimum(b, c), jnp.maximum(b, c)
    return a, b, c, d


def river_from(cards, rank):
    river = rank
    for card in sort_four(cards):
        river = river + jnp.where(river >= card, 1, 0)
    return river


def device_index():
    return lax.axis_index("board") * lax.axis_size("hand") + lax.axis_index("hand")


def send_kernel(
    turn_cards, cum_turn, opp_init, strength, cum_river, out, cum, turn_rows, root, reach, wide, sems
):
    def fetch(k):
        return pltpu.make_async_copy(cum_river.at[k], cum.at[k], sems.at[k])

    for k in range(OWNED):
        fetch(k).start()
    f32 = jnp.float32
    first_hand = device_index() * OWNED
    hand = first_hand + lax.broadcasted_iota(jnp.int32, (16, 1), 0)
    low = jnp.zeros((16, 1), jnp.int32)
    for card in range(1, 52):
        low = low + jnp.where(hand >= card * (103 - card) // 2, 1, 0)
    high = hand - ((low * (103 - low)) >> 1) + low + 1
    board = lax.broadcasted_iota(jnp.int32, (1, BOARDS), 1)
    turn = jnp.zeros((1, BOARDS), jnp.int32)
    for q in range(1, TURNS):
        turn = turn + jnp.where(board >= RIVERS * q, 1, 0)
    cards = []
    for c in range(4):
        card = jnp.zeros((1, BOARDS), jnp.int32)
        for t in range(TURNS):
            card = jnp.where(turn == t, turn_cards[t, c], card)
        cards.append(card)
    river = river_from(cards, board - RIVERS * turn)
    free = hand < LIVE
    for card in cards:
        free = free & (low != card) & (high != card)
    alive_turn = jnp.where(free, 1.0, 0.0).astype(f32)
    alive = jnp.where(free & (low != river) & (high != river), 1.0, 0.0).astype(f32)

    turn_rows[...] = jnp.zeros(turn_rows.shape, f32)
    start = opp_init[...]
    reach_map = {-1: start}
    for parent, rows in node_rows():
        picked = [cum_turn[:, row, :] for row in rows]
        summed = picked[0]
        for other in picked[1:]:
            summed = summed + other
        for row, value in zip(rows, picked):
            reach_map[row] = reach_map[parent] * (value / summed)
            turn_rows[16 * row : 16 * row + OWNED, 0:TURNS] = reach_map[row]
    lane_turn = lax.broadcasted_iota(jnp.int32, (128, BOARDS), 0)
    spread = jnp.where(lane_turn == turn, 1.0, 0.0).astype(f32)
    spread_rows = lax.dot_general(
        turn_rows[...],
        spread,
        (((1,), (0,)), ((), ())),
        precision=lax.Precision.HIGHEST,
        preferred_element_type=f32,
    )
    for line, leaf in enumerate(ENDS):
        row = REACH_ROW[leaf]
        root[line] = spread_rows[16 * row : 16 * row + 16] * alive
    owner = (board * 171) >> 9
    fold_pick = owner & 7
    folded = jnp.zeros((16, BOARDS), f32)
    for f, leaf in enumerate(FOLDS):
        row = REACH_ROW[leaf]
        folded = jnp.where(fold_pick == f, spread_rows[16 * row : 16 * row + 16], folded)
    folded = folded * alive_turn
    fold_head = folded.astype(jnp.bfloat16).astype(f32)
    fold_tail = folded - fold_head
    level = strength[...].astype(f32)
    for k in range(OWNED):
        base = k * SLOTS + LEVEL_SLOT
        reach[base : base + 1, :] = level[k : k + 1]
        reach[base + 1 : base + 2, :] = fold_head[k : k + 1]
        reach[base + 2 : base + 3, :] = fold_tail[k : k + 1]

    row_head = lax.broadcasted_iota(jnp.int32, (8, 1), 0)
    row_tail = lax.broadcasted_iota(jnp.int32, (5, 1), 0) + 8
    nodes = node_rows()

    def spread_over(row_ids, parts):
        merged = parts[-1]
        for (_, rows), part in reversed(list(zip(nodes[:-1], parts[:-1]))):
            merged = jnp.where(row_ids <= rows[-1], part, merged)
        return merged

    for k in range(OWNED):
        fetch(k).wait()
        for line in range(LINES):
            x_head = cum[k, line, 0:8, :]
            x_tail = cum[k, line, 8:13, :]
            rows = [cum[k, line, r : r + 1, :] for r in range(ROWS)]
            sums = []
            for _, ids in nodes:
                summed = rows[ids[0]]
                for r in ids[1:]:
                    summed = summed + rows[r]
                sums.append(summed)
            start = root[line, k : k + 1, :]
            q_head = x_head / spread_over(row_head, sums)
            q_tail = x_tail / spread_over(row_tail, sums)
            at_bet = start * q_head[1:2]
            at_raise = at_bet * q_head[4:5]
            at_reraise = start * q_tail[1:2]
            parents = [start, at_bet, at_raise, start, at_reraise]
            base = k * SLOTS
            reach[base + 8 * line : base + 8 * line + 8, :] = q_head * spread_over(
                row_head, parents
            )
            reach[base + 72 + 5 * line : base + 77 + 5 * line, :] = q_tail * spread_over(
                row_tail, parents
            )

    dest = lax.broadcasted_iota(jnp.int32, (DEVICES, BOARDS), 0)
    lane = lax.broadcasted_iota(jnp.int32, (DEVICES, BOARDS), 1)
    picks = [
        jnp.where(lane == LOCAL * dest + b, 1.0, 0.0).astype(jnp.bfloat16) for b in range(LOCAL)
    ]
    block_lane = lax.broadcasted_iota(jnp.int32, (DEVICES, 128), 1)

    def pick(b, values):
        return lax.dot_general(
            picks[b],
            values.astype(jnp.bfloat16),
            (((1,), (1,)), ((), ())),
            preferred_element_type=f32,
        )

    for m in range(USED_BLOCKS):
        first = 128 * m
        b = first // BOARD_SLOTS
        inside = first - b * BOARD_SLOTS
        room = min(128, BOARD_SLOTS - inside)
        part = reach[inside : inside + room, :]
        if room == 128:
            block = pick(b, part)
        elif b == LOCAL - 1:
            block = pick(b, jnp.concatenate([part, jnp.zeros((128 - room, BOARDS), f32)], 0))
        else:
            both = jnp.concatenate([part, reach[0 : 128 - room, :]], 0)
            block = jnp.where(block_lane < room, pick(b, both), pick(b + 1, both))
        wide[pl.ds(m, DEVICES, stride=BLOCKS), :] = block
    for m in range(USED_BLOCKS, BLOCKS):
        wide[pl.ds(m, DEVICES, stride=BLOCKS), :] = jnp.zeros((DEVICES, 128), f32)
    out[...] = wide[...].astype(jnp.bfloat16)


def send(turn_cards, cum_turn, opp_init, strength, cum_river):
    vmem = pl.BlockSpec(memory_space=pltpu.VMEM)
    return pl.pallas_call(
        send_kernel,
        in_specs=[
            pl.BlockSpec(memory_space=pltpu.SMEM),
            vmem,
            vmem,
            vmem,
            pl.BlockSpec(memory_space=pl.ANY),
        ],
        out_specs=vmem,
        out_shape=jax.ShapeDtypeStruct((DEVICES * BLOCKS, 128), jnp.bfloat16),
        scratch_shapes=[
            pltpu.VMEM((OWNED, LINES, ROWS, BOARDS), jnp.float32),
            pltpu.VMEM((16 * ROWS, 128), jnp.float32),
            pltpu.VMEM((LINES, 16, BOARDS), jnp.float32),
            pltpu.VMEM((BOARD_SLOTS, BOARDS), jnp.float32),
            pltpu.VMEM((DEVICES * BLOCKS, 128), jnp.float32),
            pltpu.SemaphoreType.DMA((OWNED,)),
        ],
        compiler_params=pltpu.CompilerParams(vmem_limit_bytes=VMEM),
        name="send_reach",
    )(turn_cards, cum_turn, opp_init, strength, cum_river)


def apart_kernel(marks, out):
    shared = lax.dot_general(
        marks[...], marks[...], (((1,), (1,)), ((), ())), preferred_element_type=jnp.float32
    )
    out[...] = jnp.where(shared == 0.0, 1.0, 0.0).astype(jnp.bfloat16)


def make_apart(marks):
    vmem = pl.BlockSpec(memory_space=pltpu.VMEM)
    return pl.pallas_call(
        apart_kernel,
        in_specs=[vmem],
        out_specs=vmem,
        out_shape=jax.ShapeDtypeStruct((HANDS, HANDS), jnp.bfloat16),
        compiler_params=pltpu.CompilerParams(vmem_limit_bytes=VMEM),
        name="apart_pairs",
    )(marks)


def stake_column(rows):
    line = lax.broadcasted_iota(jnp.int32, (rows, 1), 0)
    stake = jnp.zeros((rows, 1), jnp.float32)
    for i in range(rows):
        stake = jnp.where(line == i, PRE_POT + LINE_PUT[i], stake)
    return stake


def street_values(stake, end_sum, fold_sum):
    leaf_values = {}
    for leaf in ENDS:
        leaf_values[leaf] = end_sum(REACH_ROW[leaf]) * (stake + TREE[leaf]["put"][0])
    for leaf in FOLDS:
        folder = TREE[leaf]["folder"]
        lost = stake + TREE[leaf]["put"][folder]
        leaf_values[leaf] = fold_sum(REACH_ROW[leaf]) * (lost if folder == 1 else -lost)
    return back_up(leaf_values)


def board_kernel(
    turn_cards, cards, recv, apart_hbm, river_out, sums_out, apart, wide, turned, lhs, folds, marks, sem
):
    f32 = jnp.float32
    fetch = pltpu.make_async_copy(apart_hbm, apart, sem)
    fetch.start()
    wide[...] = recv[...].astype(f32)
    for m in range(USED_BLOCKS):
        block = wide[pl.ds(m, DEVICES, stride=BLOCKS), :]
        turned[128 * m : 128 * m + 128, :] = block.T
    for b in range(LOCAL):
        for k in range(OWNED):
            base = SLOTS * (OWNED * b + k)
            parts = [turned[pl.ds(base + r, 8, stride=8), :] for r in range(8)]
            parts += [turned[pl.ds(base + 72 + r, 8, stride=5), :] for r in range(5)]
            parts.append(turned[base + 64 : base + 72, :])
            parts.append(turned[base + 112 : base + 120, :])
            parts.append(jnp.zeros((8, 128), f32))
            lhs[128 * b : 128 * b + 128, 128 * k : 128 * k + 128] = jnp.concatenate(
                parts, 0
            ).astype(jnp.bfloat16)
    fetch.wait()
    folds[...] = jnp.dot(lhs[...], apart[...], preferred_element_type=f32)

    first_board = device_index() * LOCAL
    turn = first_board // RIVERS
    board_cards = [turn_cards[turn, c] for c in range(4)]
    low = cards[0:1, :]
    high = cards[1:2, :]
    free = low < 52
    for card in board_cards:
        free = free & (low != card) & (high != card)
    alive_turn = jnp.where(free, 1.0, 0.0).astype(f32)
    stake = stake_column(8)
    last_stake = PRE_POT + LINE_PUT[8]
    total = jnp.zeros((8, HANDS), f32)
    last_total = jnp.zeros((1, HANDS), f32)
    for b in range(LOCAL):
        river = river_from(board_cards, first_board + b - turn * RIVERS)
        alive = jnp.where(free & (low != river) & (high != river), 1.0, 0.0).astype(f32)
        rows = [
            turned[SLOTS * (OWNED * b + k) + LEVEL_SLOT : SLOTS * (OWNED * b + k) + LEVEL_SLOT + 1, :]
            for k in range(OWNED)
        ]
        level_row = jnp.concatenate(rows, 1).astype(jnp.bfloat16)
        signs = []
        for k in range(OWNED):
            u = SLOTS * (OWNED * b + k) + LEVEL_SLOT
            block = wide[pl.ds(u // 128, DEVICES, stride=BLOCKS), :]
            column = block[:, u % 128 : u % 128 + 1]
            column = jnp.broadcast_to(column, (DEVICES, 128)).astype(jnp.bfloat16)
            column = jnp.concatenate([column] * OWNED, 1)
            sign = jnp.clip(level_row - column, -1.0, 1.0)
            signs.append(sign * apart[128 * k : 128 * k + 128, :])
        sign = jnp.concatenate(signs, 0)
        ends = jnp.dot(lhs[128 * b : 128 * b + 128, :], sign, preferred_element_type=f32)
        values = street_values(
            stake,
            lambda r: ends[8 * r : 8 * r + 8],
            lambda r: folds[128 * b + 8 * r : 128 * b + 8 * r + 8, :],
        )
        last = street_values(
            last_stake,
            lambda r: ends[104 + r : 105 + r],
            lambda r: folds[128 * b + 104 + r : 128 * b + 105 + r, :],
        )
        values = values * alive
        last = last * alive
        river_out[b, 0:8, :] = values
        river_out[b, 8:9, :] = last
        total = total + values
        last_total = last_total + last
    fold_total = (folds[118:119, :] + folds[119:120, :]) * alive_turn
    marks[...] = jnp.zeros((128, 128), f32)
    for k in range(OWNED):
        lanes = slice(128 * k, 128 * k + 128)
        marks[8 * k : 8 * k + 8, :] = total[:, lanes]
        marks[88 + k : 89 + k, :] = last_total[:, lanes]
        marks[99 + k : 100 + k, :] = fold_total[:, lanes]
    sums_out[...] = marks[...].T


def boards(turn_cards, cards, recv, apart):
    vmem = pl.BlockSpec(memory_space=pltpu.VMEM)
    return pl.pallas_call(
        board_kernel,
        in_specs=[
            pl.BlockSpec(memory_space=pltpu.SMEM),
            vmem,
            vmem,
            pl.BlockSpec(memory_space=pl.ANY),
        ],
        out_specs=(vmem, vmem),
        out_shape=(
            jax.ShapeDtypeStruct((LOCAL, LINES, HANDS), jnp.float32),
            jax.ShapeDtypeStruct((DEVICES, 128), jnp.float32),
        ),
        scratch_shapes=[
            pltpu.VMEM((HANDS, HANDS), jnp.bfloat16),
            pltpu.VMEM((DEVICES * BLOCKS, 128), jnp.float32),
            pltpu.VMEM((DEVICES * BLOCKS, 128), jnp.float32),
            pltpu.VMEM((LOCAL * 128, HANDS), jnp.bfloat16),
            pltpu.VMEM((LOCAL * 128, HANDS), jnp.float32),
            pltpu.VMEM((128, 128), jnp.float32),
            pltpu.SemaphoreType.DMA,
        ],
        compiler_params=pltpu.CompilerParams(vmem_limit_bytes=VMEM),
        name="board_values",
    )(turn_cards, cards, recv, apart)


def turn_kernel(recv, out, turned):
    group = DEVICES // TURNS
    line_sum = jnp.zeros((TURNS, 128), jnp.float32)
    for g in range(group):
        line_sum = line_sum + recv[pl.ds(g, TURNS, stride=group), :]
    parts = [line_sum]
    for f in range(len(FOLDS)):
        parts.append(recv[pl.ds(f, TURNS, stride=group), :])
    parts.append(jnp.zeros((128 - 8 * len(parts), 128), jnp.float32))
    turned[...] = jnp.concatenate(parts, 0).T
    leaf_values = {}
    for line, leaf in enumerate(ENDS):
        if line < 8:
            value = turned[pl.ds(line, OWNED, stride=8), :]
        else:
            value = turned[88 : 88 + OWNED, :]
        leaf_values[leaf] = value[:, 0:TURNS] / float(RIVERS)
    folds = turned[99 : 99 + OWNED, :]
    for f, leaf in enumerate(FOLDS):
        folder = TREE[leaf]["folder"]
        lost = PRE_POT + TREE[leaf]["put"][folder]
        leaf_values[leaf] = folds[:, 8 * f + 8 : 8 * f + 16] * (lost if folder == 1 else -lost)
    out[...] = back_up(leaf_values)


def turns(recv):
    vmem = pl.BlockSpec(memory_space=pltpu.VMEM)
    return pl.pallas_call(
        turn_kernel,
        in_specs=[vmem],
        out_specs=vmem,
        out_shape=jax.ShapeDtypeStruct((OWNED, TURNS), jnp.float32),
        scratch_shapes=[pltpu.VMEM((128, 128), jnp.float32)],
        name="turn_values",
    )(recv)


def body(cum_turn, cum_river, opp_init, turn_cards, strength):
    low, high = hand_cards(HANDS)
    order = np.arange(HANDS).reshape(DEVICES, OWNED).T.reshape(-1)
    low, high = low[order], high[order]
    cards = np.zeros((8, HANDS), np.int32)
    cards[0], cards[1] = low, high
    deck = np.arange(128)
    marks = ((low[:, None] == deck) | (high[:, None] == deck)).astype(np.float32)

    packed = send(turn_cards, cum_turn, opp_init, strength, cum_river)
    packed = packed.reshape(DEVICES, BLOCKS, 128)
    recv = lax.all_to_all(packed, AXES, split_axis=0, concat_axis=0, tiled=True)
    apart = make_apart(jnp.asarray(marks, jnp.bfloat16))
    river, sums = boards(
        turn_cards, jnp.asarray(cards), recv.reshape(DEVICES * BLOCKS, 128), apart
    )
    back = lax.all_to_all(
        sums.reshape(DEVICES, 1, 128), AXES, split_axis=0, concat_axis=0, tiled=True
    )
    river = river.reshape(LOCAL, LINES, OWNED, DEVICES)
    river_value = jnp.transpose(river, (0, 1, 3, 2)).reshape(LOCAL, LINES, HANDS)
    return river_value, turns(back.reshape(DEVICES, 128))


def solution(mesh):
    placed = (
        P(AXES, None, None),
        P(AXES, None, None, None),
        P(AXES, None),
        P(),
        P(AXES, None),
    )
    return jax.shard_map(
        body,
        mesh=mesh,
        in_specs=placed,
        out_specs=(P(AXES, None, None), P(AXES, None)),
        check_vma=False,
    )
```

time: 492 us -> 72.6 us (0.15); the launches traced: 485 us -> 72 us
  local copies, waits for them, and re-layouts: 139 us -> 10.6 us
  waiting for transfers between devices: 146 us -> 22 us
  blocking collectives: 90.6 us -> 0 us
  other arithmetic: 38.3 us -> 0 us
  matrix products: 28.7 us -> 0 us
  Pallas kernels: 0 us -> 23.2 us
  between operations: 15.1 us -> 0.68 us
  starting transfers between devices: 26.3 us -> 15.5 us
    psum x1 -> x0, waiting for transfers between devices: 140 us -> none  [body(): summed_all = lax.psum(partial_value, ('board', 'hand'))]
    psum x1 -> x0, blocking collectives: 90.6 us -> none  [body(): lax.psum((card_sums, fold_totals), ('board', 'hand'))]
    unnamed x113 -> x8, local copies, waits for them, and re-layouts: 64 us -> 7.24 us
    another operation x19 -> x0, local copies, waits for them, and re-layouts: 45.7 us -> none  [the longest x2 23.6 us: to_owners(): packed = packed.reshape(owned, row_width, device_count, local_boards)]
    another operation x5 -> x0, other arithmetic: 29.8 us -> none  [the longest x2 23.8 us: settle_rows(): jnp.stack([reach_map[leaf_id] for leaf_id in end_leaves + fold_leaves], a...]
    dot_general x7 -> x0, matrix products: 28.3 us -> none  [the longest x3 16.2 us: board_values(): lax.dot_general(end_rows, sign_matrix, contract, preferred_element_type=j...]
    pallas_call x0 -> x4, Pallas kernels: none -> 23.2 us  [the longest x1 9.73 us: boards(): pl.pallas_call(board_kernel, in_specs=[pl.BlockSpec(memory_space=pltpu.SM...]
    all_to_all x3 -> x2, waiting for transfers between devices: 5.7 us -> 22 us  [the longest x1 15.4 us: body(): recv = lax.all_to_all(packed, AXES, split_axis=0, concat_axis=0, tiled=True)]
  transfers between devices with their start and end apart: 4 -> 2, of which waited for: 2 -> 2; matrix products, arithmetic and copies ran while one was open for 12% -> 5% of each run, Pallas kernels for 0% -> 6%
where the time goes in v1:
time: 72.6 us; the launch traced here: 72 us
  Pallas kernels  23.2 us (32%)
  waiting for transfers between devices  22 us (30%)
  starting transfers between devices  15.5 us (21%)
  local copies, waits for them, and re-layouts  10.6 us (15%)
    all_to_all x1, waiting for transfers between devices, body(): recv = lax.all_to_all(packed, AXES, split_axis=0, concat_axis=0, tiled=True)  15.4 us
    all_to_all x1, starting transfers between devices, body(): recv = lax.all_to_all(packed, AXES, split_axis=0, concat_axis=0, tiled=True)  11.5 us
    pallas_call x1, Pallas kernels, boards(): pl.pallas_call(board_kernel, in_specs=[pl.BlockSpec(memory_space=pltpu.SM...  9.73 us
    pallas_call x1, Pallas kernels, send(): pl.pallas_call(send_kernel, in_specs=[pl.BlockSpec(memory_space=pltpu.SME...  7.56 us
    unnamed x8, local copies, waits for them, and re-layouts  7.24 us
    all_to_all x1, waiting for transfers between devices, body(): lax.all_to_all(sums.reshape(DEVICES, 1, 128), AXES, split_axis=0, concat_...  6.56 us
    pallas_call x1, Pallas kernels, make_apart(): pl.pallas_call(apart_kernel, in_specs=[vmem], out_specs=vmem, out_shape=j...  4.06 us
    all_to_all x1, starting transfers between devices, body(): lax.all_to_all(sums.reshape(DEVICES, 1, 128), AXES, split_axis=0, concat_...  4.02 us
  transfers between devices with their start and end apart: 2, of which 2 were waited for; matrix products, arithmetic and copies ran while one was open for 5% of the time, Pallas kernels for 6%

profile of v1, /device:TPU:1, one launch (start us, length us, event | category | flops | bytes accessed | tf_op | source)
XLA Modules:
  0.0 72.0 jit_solution(9633871151881809359)
XLA Ops:
  0.6 1.3 %copy.25.turn_cards = s32[8,4]{1,0:T(8,128)} copy(s32[8,4]{0,1:T(4,128)} %param.10) | data formatting | bytes 256 | tf_op args[3]
  2.0 1.4 %copy.24.opp_init = f32[11,8]{1,0:T(8,128)} copy(f32[11,8]{0,1:T(8,128)} %param.9) | data formatting | bytes 704 | tf_op args[2]
  3.3 1.6 %copy.23.cum_turn = f32[11,13,8]{2,1,0:T(8,128)} copy(f32[11,13,8]{1,2,0:T(8,128)} %param.7) | data formatting | bytes 9152 | tf_op args[0]
  4.9 7.6 %send_reach.1 = bf16[4096,128]{1,0:T(8,128)(2,1)} custom-call(s32[8,4]{1,0:T(8,128)} %copy.25.turn_cards, f32[11,13,8]{2,1,0:T(8,128)} %copy.23.cum_turn, f32[11,8]{1,0:T(8,128)} %copy.24.opp_init, s32[11,384]{1,0:T(8,128)} %strength.1, f32[11,9,13,384]{3,2,1,0:T(8,128)} %cum_river.1), custom_call_target="tpu_custom_call" | custom-call | tf_op jit(solution)/shard_map/send_reach/pallas_call | solution.py:297
  12.5 11.5 %all-to-all-start = ((bf16[128,32,128]{2,1,0:T(8,128)(2,1)}), bf16[128,32,128]{2,1,0:T(8,128)(2,1)S(1)}, u32[]{:S(2)}, u32[]{:S(2)}) async-start(bf16[128,32,128]{2,1,0:T(8,128)(2,1)} %bitcast.13), calls=%async_computation | async-start | bytes 2097152 | tf_op jit(solution)/shard_map/all_to_all | solution.py:518
  24.0 4.1 %apart_pairs.1.apart_hbm = bf16[1408,1408]{1,0:T(8,128)(2,1)} custom-call(bf16[1408,128]{1,0:T(8,128)(2,1)} %constant.4.clone.marks), custom_call_target="tpu_custom_call" | custom-call | tf_op jit(solution)/shard_map/apart_pairs/pallas_call | solution.py:330
  28.1 15.4 %all-to-all-done = bf16[128,32,128]{2,1,0:T(8,128)(2,1)S(1)} async-done(((bf16[128,32,128]{2,1,0:T(8,128)(2,1)}), bf16[128,32,128]{2,1,0:T(8,128)(2,1)S(1)}, u32[]{:S(2)}, u32[]{:S(2)}) %all-to-all-start) | async-done | bytes 1048608 | tf_op jit(solution)/shard_map/all_to_all | solution.py:518
  43.5 0.0 copy-start
  43.5 1.0 %copy-done = bf16[128,32,128]{2,1,0:T(8,128)(2,1)} copy-done((bf16[128,32,128]{2,1,0:T(8,128)(2,1)}, bf16[128,32,128]{2,1,0:T(8,128)(2,1)S(1)}, u32[]{:S(2)}) %copy-start) | copy-done | bytes 1048600
  44.5 9.7 %board_values.1 = (f32[3,9,1408]{2,1,0:T(8,128)}, f32[128,128]{1,0:T(8,128)}) custom-call(s32[8,4]{1,0:T(8,128)} %copy.25.turn_cards, s32[8,1408]{1,0:T(8,128)} %constant.5.clone.cards, bf16[4096,128]{1,0:T(8,128)(2,1)} %bitcast.12, bf16[1408,1408]{1,0:T(8,128)(2,1)} %apart_pairs.1.apart_hbm), custom_call_target="tpu_custom_call" | custom-call | tf_op jit(solution)/shard_map/board_values/pallas_call | solution.py:443
  54.2 4.0 %all-to-all-start.1 = ((f32[128,1,128]{2,1,0:T(1,128)}), f32[128,1,128]{2,1,0:T(1,128)S(1)}, u32[]{:S(2)}, u32[]{:S(2)}) async-start(f32[128,1,128]{2,1,0:T(1,128)} %bitcast.16), calls=%async_computation.1 | async-start | bytes 131072 | tf_op jit(solution)/shard_map/all_to_all | solution.py:523
  58.2 1.0 %reshape.28 = f32[3,9,11,128]{3,2,1,0:T(8,128)S(1)} reshape(f32[3,9,1408]{2,1,0:T(8,128)} %get-tuple-element.4) | data formatting | bytes 304128 | tf_op jit(solution)/shard_map/reshape | solution.py:526
  59.2 0.6 copy.27
  59.8 1.7 %reshape.25 = f32[3,9,1408]{2,0,1:T(4,128)} reshape(f32[3,9,128,11]{3,2,0,1:T(8,128)S(1)} %copy.27) | data formatting | bytes 304128 | tf_op jit(solution)/shard_map/reshape | solution.py:527
  61.6 6.6 %all-to-all-done.1 = f32[128,1,128]{2,1,0:T(1,128)S(1)} async-done(((f32[128,1,128]{2,1,0:T(1,128)}), f32[128,1,128]{2,1,0:T(1,128)S(1)}, u32[]{:S(2)}, u32[]{:S(2)}) %all-to-all-start.1) | async-done | bytes 65568 | tf_op jit(solution)/shard_map/all_to_all | solution.py:523
  68.1 0.0 copy-start.1
  68.1 0.6 copy-done.1
  68.8 1.9 %turn_values.1 = f32[11,8]{1,0:T(8,128)} custom-call(f32[128,128]{1,0:T(8,128)} %bitcast.15), custom_call_target="tpu_custom_call" | custom-call | tf_op jit(solution)/shard_map/turn_values/pallas_call | solution.py:497
  70.7 1.4 %copy.29 = f32[11,8]{0,1:T(8,128)} copy(f32[11,8]{1,0:T(8,128)} %turn_values.1) | data formatting | bytes 704
Async XLA Ops:
  12.5 31.0 %all-to-all-start = ((bf16[128,32,128]{2,1,0:T(8,128)(2,1)}), bf16[128,32,128]{2,1,0:T(8,128)(2,1)S(1)}, u32[]{:S(2)}, u32[]{:S(2)}) async-start(bf16[128,32,128]{2,1,0:T(8,128)(2,1)} %bitcast.13), calls=%async_computation | async-start | bytes 2097152 | tf_op jit(solution)/shard_map/all_to_all | solution.py:518
  43.5 1.0 %copy-start = (bf16[128,32,128]{2,1,0:T(8,128)(2,1)}, bf16[128,32,128]{2,1,0:T(8,128)(2,1)S(1)}, u32[]{:S(2)}) copy-start(bf16[128,32,128]{2,1,0:T(8,128)(2,1)S(1)} %all-to-all-done) | copy-start | bytes 3145732
  54.2 13.9 %all-to-all-start.1 = ((f32[128,1,128]{2,1,0:T(1,128)}), f32[128,1,128]{2,1,0:T(1,128)S(1)}, u32[]{:S(2)}, u32[]{:S(2)}) async-start(f32[128,1,128]{2,1,0:T(1,128)} %bitcast.16), calls=%async_computation.1 | async-start | bytes 131072 | tf_op jit(solution)/shard_map/all_to_all | solution.py:523
  68.1 0.6 copy-start.1

commit v2 on v1

--- a/solution.py
+++ b/solution.py
@@ -10,6 +10,7 @@
 RIVERS = 48
 BETS = 4
 PRE_POT = 2.0
+UNROLL = True
 AXES = ("board", "hand")
 
 HANDS = 1408
@@ -20,12 +21,14 @@
 BOARDS = 384
 TURNS = 8
 LOCAL = BOARDS // DEVICES
-SLOTS = 120
+SLOTS = 88
 BOARD_SLOTS = OWNED * SLOTS
-BLOCKS = 32
-USED_BLOCKS = 31
-LEVEL_SLOT = 117
-VMEM = 56 * 1024 * 1024
+BLOCKS = 24
+USED_BLOCKS = 23
+PITCH = 24
+BOARD_ROWS = 96
+LEVEL_SLOT = 81
+VMEM = 48 * 1024 * 1024
 
 
 def grow_street(bet_cap):
@@ -91,6 +94,9 @@
             REACH_ROW[_child] = REACH_ROW[_i]
 LINE_PUT = [TREE[i]["put"][0] for i in ENDS]
 
+SENT = [10, 11, 2, 3, 8, 5, 6, 7, 12]
+SUM_OF = {4: ([5, 6], []), 9: ([10, 11, 12], []), 1: ([2, 3, 4], []), 0: ([7, 8, 9], [1])}
+
 
 def hand_cards(hand_count):
     card_low = []
@@ -173,7 +179,7 @@
     for c in range(4):
         card = jnp.zeros((1, BOARDS), jnp.int32)
         for t in range(TURNS):
-            card = jnp.where(turn == t, turn_cards[t, c], card)
+            card = jnp.where(turn == t, turn_cards[c, t], card)
         cards.append(card)
     river = river_from(cards, board - RIVERS * turn)
     free = hand < LIVE
@@ -183,25 +189,38 @@
     alive = jnp.where(free & (low != river) & (high != river), 1.0, 0.0).astype(f32)
 
     turn_rows[...] = jnp.zeros(turn_rows.shape, f32)
-    start = opp_init[...]
-    reach_map = {-1: start}
+    turn_rows[0 : OWNED * TURNS, 0:ROWS] = cum_turn[...].reshape(OWNED * TURNS, ROWS)
+    turn_rows[128 : 128 + TURNS, 0:OWNED] = opp_init[...]
+    by_row = turn_rows[0:128, :].T
+    start = turn_rows[128:256, :].T[0:16]
+    reach_map = {-1: None}
+    lane = lax.broadcasted_iota(jnp.int32, (16, 128), 1)
+    own = (lane >> 3) == lax.broadcasted_iota(jnp.int32, (16, 128), 0)
+    stacked = [start]
     for parent, rows in node_rows():
-        picked = [cum_turn[:, row, :] for row in rows]
+        picked = [by_row[row : row + 1] for row in rows]
         summed = picked[0]
         for other in picked[1:]:
             summed = summed + other
         for row, value in zip(rows, picked):
-            reach_map[row] = reach_map[parent] * (value / summed)
-            turn_rows[16 * row : 16 * row + OWNED, 0:TURNS] = reach_map[row]
+            share = value / summed
+            reach_map[row] = share if parent < 0 else reach_map[parent] * share
+    for row in range(ROWS):
+        stacked.append(jnp.where(own, reach_map[row], 0.0))
     lane_turn = lax.broadcasted_iota(jnp.int32, (128, BOARDS), 0)
-    spread = jnp.where(lane_turn == turn, 1.0, 0.0).astype(f32)
-    spread_rows = lax.dot_general(
-        turn_rows[...],
+    spread = jnp.where((lane_turn & 7) == turn, 1.0, 0.0).astype(f32)
+    spread = jnp.where(lane_turn < OWNED * TURNS, spread, 0.0)
+    spread_all = lax.dot_general(
+        jnp.concatenate(stacked, 0),
         spread,
         (((1,), (0,)), ((), ())),
         precision=lax.Precision.HIGHEST,
         preferred_element_type=f32,
     )
+    opponent = spread_all[0:16]
+    alive_turn = alive_turn * opponent
+    alive = alive * opponent
+    spread_rows = spread_all[16:]
     for line, leaf in enumerate(ENDS):
         row = REACH_ROW[leaf]
         root[line] = spread_rows[16 * row : 16 * row + 16] * alive
@@ -216,13 +235,13 @@
     fold_tail = folded - fold_head
     level = strength[...].astype(f32)
     for k in range(OWNED):
-        base = k * SLOTS + LEVEL_SLOT
-        reach[base : base + 1, :] = level[k : k + 1]
-        reach[base + 1 : base + 2, :] = fold_head[k : k + 1]
-        reach[base + 2 : base + 3, :] = fold_tail[k : k + 1]
+        reach[k, 80:88, :] = jnp.zeros((8, BOARDS), f32)
+        reach[k, 81:82, :] = level[k : k + 1]
+        reach[k, 82:83, :] = fold_head[k : k + 1]
+        reach[k, 83:84, :] = fold_tail[k : k + 1]
 
     row_head = lax.broadcasted_iota(jnp.int32, (8, 1), 0)
-    row_tail = lax.broadcasted_iota(jnp.int32, (5, 1), 0) + 8
+    row_tail = lax.broadcasted_iota(jnp.int32, (8, 1), 0) + 8
     nodes = node_rows()
 
     def spread_over(row_ids, parts):
@@ -231,11 +250,11 @@
             merged = jnp.where(row_ids <= rows[-1], part, merged)
         return merged
 
-    for k in range(OWNED):
+    def one_hand(k, carry):
         fetch(k).wait()
         for line in range(LINES):
             x_head = cum[k, line, 0:8, :]
-            x_tail = cum[k, line, 8:13, :]
+            x_tail = jnp.concatenate([cum[k, line, 8:13, :], jnp.ones((3, BOARDS), f32)], 0)
             rows = [cum[k, line, r : r + 1, :] for r in range(ROWS)]
             sums = []
             for _, ids in nodes:
@@ -243,20 +262,25 @@
                 for r in ids[1:]:
                     summed = summed + rows[r]
                 sums.append(summed)
-            start = root[line, k : k + 1, :]
+            start = root[line, pl.ds(k, 1), :]
             q_head = x_head / spread_over(row_head, sums)
             q_tail = x_tail / spread_over(row_tail, sums)
             at_bet = start * q_head[1:2]
             at_raise = at_bet * q_head[4:5]
             at_reraise = start * q_tail[1:2]
             parents = [start, at_bet, at_raise, start, at_reraise]
-            base = k * SLOTS
-            reach[base + 8 * line : base + 8 * line + 8, :] = q_head * spread_over(
-                row_head, parents
+            head = q_head * spread_over(row_head, parents)
+            tail = q_tail * spread_over(row_tail, parents)
+            mixed = jnp.where(
+                row_head < 2,
+                pltpu.roll(tail, 6, 0),
+                jnp.where(row_head == 4, pltpu.roll(tail, 4, 0), head),
             )
-            reach[base + 72 + 5 * line : base + 77 + 5 * line, :] = q_tail * spread_over(
-                row_tail, parents
-            )
+            reach[k, 8 * line : 8 * line + 8, :] = mixed
+            reach[k, 72 + line : 73 + line, :] = tail[4:5]
+        return carry
+
+    lax.fori_loop(0, OWNED, one_hand, 0, unroll=True)
 
     dest = lax.broadcasted_iota(jnp.int32, (DEVICES, BOARDS), 0)
     lane = lax.broadcasted_iota(jnp.int32, (DEVICES, BOARDS), 1)
@@ -273,27 +297,43 @@
             preferred_element_type=f32,
         )
 
-    for m in range(USED_BLOCKS):
-        first = 128 * m
-        b = first // BOARD_SLOTS
-        inside = first - b * BOARD_SLOTS
-        room = min(128, BOARD_SLOTS - inside)
-        part = reach[inside : inside + room, :]
-        if room == 128:
-            block = pick(b, part)
-        elif b == LOCAL - 1:
-            block = pick(b, jnp.concatenate([part, jnp.zeros((128 - room, BOARDS), f32)], 0))
+    flat = reach.reshape(BOARD_SLOTS, BOARDS)
+
+    def put(m, block):
+        wide.reshape(DEVICES * PITCH, 128)[pl.ds(m, DEVICES, stride=PITCH), :] = block
+
+    for b in range(LOCAL):
+        first = -(-b * BOARD_SLOTS // 128)
+        last = (b + 1) * BOARD_SLOTS // 128
+
+        def whole_block(m, carry):
+            start = pl.multiple_of(128 * m - b * BOARD_SLOTS, 8)
+            put(m, pick(b, flat[pl.ds(start, 128), :]))
+            return carry
+
+        lax.fori_loop(first, last, whole_block, 0, unroll=UNROLL)
+        inside = 128 * last - b * BOARD_SLOTS
+        room = BOARD_SLOTS - inside
+        part = flat[inside:BOARD_SLOTS, :]
+        if b == LOCAL - 1:
+            put(last, pick(b, jnp.concatenate([part, jnp.zeros((128 - room, BOARDS), f32)], 0)))
         else:
-            both = jnp.concatenate([part, reach[0 : 128 - room, :]], 0)
-            block = jnp.where(block_lane < room, pick(b, both), pick(b + 1, both))
-        wide[pl.ds(m, DEVICES, stride=BLOCKS), :] = block
+            both = jnp.concatenate([part, flat[0 : 128 - room, :]], 0)
+            put(last, jnp.where(block_lane < room, pick(b, both), pick(b + 1, both)))
     for m in range(USED_BLOCKS, BLOCKS):
-        wide[pl.ds(m, DEVICES, stride=BLOCKS), :] = jnp.zeros((DEVICES, 128), f32)
-    out[...] = wide[...].astype(jnp.bfloat16)
+        put(m, jnp.zeros((DEVICES, 128), f32))
+    out[...] = wide[:, 0:BLOCKS, :].astype(jnp.bfloat16).reshape(DEVICES * BLOCKS, 128)
+
+
+def keep(space, *arrays):
+    return [pltpu.with_memory_space_constraint(array, space) for array in arrays]
 
 
 def send(turn_cards, cum_turn, opp_init, strength, cum_river):
     vmem = pl.BlockSpec(memory_space=pltpu.VMEM)
+    turn_cards, cum_turn, opp_init, strength, cum_river = keep(
+        pltpu.HBM, turn_cards, cum_turn, opp_init, strength, cum_river
+    )
     return pl.pallas_call(
         send_kernel,
         in_specs=[
@@ -304,13 +344,13 @@
             pl.BlockSpec(memory_space=pl.ANY),
         ],
         out_specs=vmem,
-        out_shape=jax.ShapeDtypeStruct((DEVICES * BLOCKS, 128), jnp.bfloat16),
+        out_shape=pltpu.VMEM((DEVICES * BLOCKS, 128), jnp.bfloat16),
         scratch_shapes=[
             pltpu.VMEM((OWNED, LINES, ROWS, BOARDS), jnp.float32),
-            pltpu.VMEM((16 * ROWS, 128), jnp.float32),
+            pltpu.VMEM((256, 128), jnp.float32),
             pltpu.VMEM((LINES, 16, BOARDS), jnp.float32),
-            pltpu.VMEM((BOARD_SLOTS, BOARDS), jnp.float32),
-            pltpu.VMEM((DEVICES * BLOCKS, 128), jnp.float32),
+            pltpu.VMEM((OWNED, SLOTS, BOARDS), jnp.float32),
+            pltpu.VMEM((DEVICES, PITCH, 128), jnp.float32),
             pltpu.SemaphoreType.DMA((OWNED,)),
         ],
         compiler_params=pltpu.CompilerParams(vmem_limit_bytes=VMEM),
@@ -327,11 +367,12 @@
 
 def make_apart(marks):
     vmem = pl.BlockSpec(memory_space=pltpu.VMEM)
+    (marks,) = keep(pltpu.HBM, marks)
     return pl.pallas_call(
         apart_kernel,
         in_specs=[vmem],
         out_specs=vmem,
-        out_shape=jax.ShapeDtypeStruct((HANDS, HANDS), jnp.bfloat16),
+        out_shape=pltpu.HBM((HANDS, HANDS), jnp.bfloat16),
         compiler_params=pltpu.CompilerParams(vmem_limit_bytes=VMEM),
         name="apart_pairs",
     )(marks)
@@ -345,44 +386,112 @@
     return stake
 
 
-def street_values(stake, end_sum, fold_sum):
+def all_rows(sums):
+    sums = dict(sums)
+    for row, (plus, minus) in SUM_OF.items():
+        total = sums[plus[0]]
+        for other in plus[1:]:
+            total = total + sums[other]
+        for other in minus:
+            total = total - sums[other]
+        sums[row] = total
+    return sums
+
+
+def street_values(stake, end_sums, fold_sums):
+    end_sums = all_rows(end_sums)
+    fold_sums = all_rows(fold_sums)
     leaf_values = {}
     for leaf in ENDS:
-        leaf_values[leaf] = end_sum(REACH_ROW[leaf]) * (stake + TREE[leaf]["put"][0])
+        leaf_values[leaf] = end_sums[REACH_ROW[leaf]] * (stake + TREE[leaf]["put"][0])
     for leaf in FOLDS:
         folder = TREE[leaf]["folder"]
         lost = stake + TREE[leaf]["put"][folder]
-        leaf_values[leaf] = fold_sum(REACH_ROW[leaf]) * (lost if folder == 1 else -lost)
+        leaf_values[leaf] = fold_sums[REACH_ROW[leaf]] * (lost if folder == 1 else -lost)
     return back_up(leaf_values)
 
 
 def board_kernel(
-    turn_cards, cards, recv, apart_hbm, river_out, sums_out, apart, wide, turned, lhs, folds, marks, sem
+    turn_cards,
+    cards,
+    recv,
+    apart_hbm,
+    marks_in_hbm,
+    marks_out_hbm,
+    river_out,
+    sums_out,
+    apart,
+    marks_in,
+    marks_out,
+    wide,
+    turned,
+    lhs,
+    columns,
+    ends,
+    folds,
+    marks,
+    sems,
 ):
     f32 = jnp.float32
-    fetch = pltpu.make_async_copy(apart_hbm, apart, sem)
-    fetch.start()
-    wide[...] = recv[...].astype(f32)
-    for m in range(USED_BLOCKS):
-        block = wide[pl.ds(m, DEVICES, stride=BLOCKS), :]
-        turned[128 * m : 128 * m + 128, :] = block.T
+    bf16 = jnp.bfloat16
+    loads = [
+        pltpu.make_async_copy(marks_in_hbm, marks_in, sems.at[0]),
+        pltpu.make_async_copy(marks_out_hbm, marks_out, sems.at[1]),
+        pltpu.make_async_copy(apart_hbm, apart, sems.at[2]),
+    ]
+    for load in loads:
+        load.start()
+    wide[:, 0:BLOCKS, :] = recv[...].astype(f32).reshape(DEVICES, BLOCKS, 128)
+
+    def turn_block(m, carry):
+        block = wide.reshape(DEVICES * PITCH, 128)[pl.ds(m, DEVICES, stride=PITCH), :]
+        turned[pl.ds(pl.multiple_of(128 * m, 128), 128), :] = block.T
+        return carry
+
+    lax.fori_loop(0, USED_BLOCKS, turn_block, 0, unroll=UNROLL)
+
     for b in range(LOCAL):
-        for k in range(OWNED):
-            base = SLOTS * (OWNED * b + k)
-            parts = [turned[pl.ds(base + r, 8, stride=8), :] for r in range(8)]
-            parts += [turned[pl.ds(base + 72 + r, 8, stride=5), :] for r in range(5)]
-            parts.append(turned[base + 64 : base + 72, :])
-            parts.append(turned[base + 112 : base + 120, :])
+
+        def one_hand(k, carry):
+            base = pl.multiple_of(SLOTS * (OWNED * b + k), 8)
+            lanes = pl.ds(pl.multiple_of(128 * k, 128), 128)
+            parts = [turned[pl.ds(base + g, 8, stride=8), :] for g in range(8)]
+            for first in (72, 64, 80):
+                parts.append(turned[pl.ds(base + first, 8), :])
             parts.append(jnp.zeros((8, 128), f32))
-            lhs[128 * b : 128 * b + 128, 128 * k : 128 * k + 128] = jnp.concatenate(
-                parts, 0
-            ).astype(jnp.bfloat16)
-    fetch.wait()
-    folds[...] = jnp.dot(lhs[...], apart[...], preferred_element_type=f32)
+            lhs[BOARD_ROWS * b : BOARD_ROWS * (b + 1), lanes] = jnp.concatenate(parts, 0).astype(
+                bf16
+            )
+            return carry
+
+        lax.fori_loop(0, OWNED, one_hand, 0, unroll=UNROLL)
+
+    level_rows = jnp.concatenate(
+        [
+            turned[pl.ds(LEVEL_SLOT, LOCAL * OWNED, stride=SLOTS), :],
+            jnp.zeros((128 - LOCAL * OWNED, 128), f32),
+        ],
+        0,
+    )
+    level_columns = level_rows.T
+    for q in range(LOCAL * OWNED):
+        column = level_columns[:, q : q + 1]
+        columns[q] = jnp.broadcast_to(column, (DEVICES, 128)).astype(bf16)
+
+    loads[0].wait()
+    loads[1].wait()
+    card_sums = jnp.dot(lhs[...], marks_in[...], preferred_element_type=f32)
+    lane = lax.broadcasted_iota(jnp.int32, card_sums.shape, 1)
+    head = card_sums.astype(bf16).astype(f32)
+    middle = (card_sums - head).astype(bf16).astype(f32)
+    tail = card_sums - head - middle
+    split = jnp.where(lane < 64, head, jnp.where(lane < 128, middle, tail)).astype(bf16)
+    folds[...] = jnp.dot(split, marks_out[...], preferred_element_type=f32) + lhs[...].astype(f32)
+    loads[2].wait()
 
     first_board = device_index() * LOCAL
     turn = first_board // RIVERS
-    board_cards = [turn_cards[turn, c] for c in range(4)]
+    board_cards = [turn_cards[c, turn] for c in range(4)]
     low = cards[0:1, :]
     high = cards[1:2, :]
     free = low < 52
@@ -396,39 +505,45 @@
     for b in range(LOCAL):
         river = river_from(board_cards, first_board + b - turn * RIVERS)
         alive = jnp.where(free & (low != river) & (high != river), 1.0, 0.0).astype(f32)
-        rows = [
-            turned[SLOTS * (OWNED * b + k) + LEVEL_SLOT : SLOTS * (OWNED * b + k) + LEVEL_SLOT + 1, :]
+        row_tiles = [
+            jnp.concatenate(
+                [jnp.broadcast_to(level_rows[OWNED * b + k : OWNED * b + k + 1], (16, 128))] * 8, 0
+            ).astype(bf16)
             for k in range(OWNED)
         ]
-        level_row = jnp.concatenate(rows, 1).astype(jnp.bfloat16)
-        signs = []
-        for k in range(OWNED):
-            u = SLOTS * (OWNED * b + k) + LEVEL_SLOT
-            block = wide[pl.ds(u // 128, DEVICES, stride=BLOCKS), :]
-            column = block[:, u % 128 : u % 128 + 1]
-            column = jnp.broadcast_to(column, (DEVICES, 128)).astype(jnp.bfloat16)
-            column = jnp.concatenate([column] * OWNED, 1)
-            sign = jnp.clip(level_row - column, -1.0, 1.0)
-            signs.append(sign * apart[128 * k : 128 * k + 128, :])
-        sign = jnp.concatenate(signs, 0)
-        ends = jnp.dot(lhs[128 * b : 128 * b + 128, :], sign, preferred_element_type=f32)
-        values = street_values(
-            stake,
-            lambda r: ends[8 * r : 8 * r + 8],
-            lambda r: folds[128 * b + 8 * r : 128 * b + 8 * r + 8, :],
-        )
-        last = street_values(
-            last_stake,
-            lambda r: ends[104 + r : 105 + r],
-            lambda r: folds[128 * b + 104 + r : 128 * b + 105 + r, :],
-        )
+        rows = slice(BOARD_ROWS * b, BOARD_ROWS * (b + 1))
+        for first in range(0, OWNED, 2):
+            tiles = range(first, min(first + 2, OWNED))
+            lanes = slice(128 * first, 128 * (tiles[-1] + 1))
+            signs = []
+            for k in range(OWNED):
+                column = columns[OWNED * b + k]
+                pieces = []
+                for i in tiles:
+                    pair = apart[128 * k : 128 * k + 128, 128 * i : 128 * i + 128]
+                    pieces.append(jnp.clip(row_tiles[i] - column, -1.0, 1.0) * pair)
+                signs.append(jnp.concatenate(pieces, 1))
+            sign = jnp.concatenate(signs, 0)
+            ends[rows, lanes] = jnp.dot(lhs[rows, :], sign, preferred_element_type=f32)
+        base = BOARD_ROWS * b
+
+        def main_rows(sums):
+            return {
+                r: sums[base + 8 * i : base + 8 * i + 8, :] for i, r in enumerate(SENT)
+            }
+
+        def last_rows(sums):
+            return {r: sums[base + 72 + i : base + 73 + i, :] for i, r in enumerate(SENT)}
+
+        values = street_values(stake, main_rows(ends), main_rows(folds))
+        last = street_values(last_stake, last_rows(ends), last_rows(folds))
         values = values * alive
         last = last * alive
         river_out[b, 0:8, :] = values
         river_out[b, 8:9, :] = last
         total = total + values
         last_total = last_total + last
-    fold_total = (folds[118:119, :] + folds[119:120, :]) * alive_turn
+    fold_total = (folds[82:83, :] + folds[83:84, :]) * alive_turn
     marks[...] = jnp.zeros((128, 128), f32)
     for k in range(OWNED):
         lanes = slice(128 * k, 128 * k + 128)
@@ -438,36 +553,40 @@
     sums_out[...] = marks[...].T
 
 
-def boards(turn_cards, cards, recv, apart):
+def boards(turn_cards, cards, recv, apart, marks_in, marks_out):
     vmem = pl.BlockSpec(memory_space=pltpu.VMEM)
+    hbm = pl.BlockSpec(memory_space=pl.ANY)
+    (recv,) = keep(pltpu.VMEM, recv)
+    turn_cards, cards, apart, marks_in, marks_out = keep(
+        pltpu.HBM, turn_cards, cards, apart, marks_in, marks_out
+    )
     return pl.pallas_call(
         board_kernel,
-        in_specs=[
-            pl.BlockSpec(memory_space=pltpu.SMEM),
-            vmem,
-            vmem,
-            pl.BlockSpec(memory_space=pl.ANY),
-        ],
+        in_specs=[pl.BlockSpec(memory_space=pltpu.SMEM), vmem, vmem, hbm, hbm, hbm],
         out_specs=(vmem, vmem),
         out_shape=(
             jax.ShapeDtypeStruct((LOCAL, LINES, HANDS), jnp.float32),
-            jax.ShapeDtypeStruct((DEVICES, 128), jnp.float32),
+            pltpu.VMEM((DEVICES, 128), jnp.float32),
         ),
         scratch_shapes=[
             pltpu.VMEM((HANDS, HANDS), jnp.bfloat16),
+            pltpu.VMEM((HANDS, 256), jnp.bfloat16),
+            pltpu.VMEM((256, HANDS), jnp.bfloat16),
+            pltpu.VMEM((DEVICES, PITCH, 128), jnp.float32),
             pltpu.VMEM((DEVICES * BLOCKS, 128), jnp.float32),
-            pltpu.VMEM((DEVICES * BLOCKS, 128), jnp.float32),
-            pltpu.VMEM((LOCAL * 128, HANDS), jnp.bfloat16),
-            pltpu.VMEM((LOCAL * 128, HANDS), jnp.float32),
+            pltpu.VMEM((LOCAL * BOARD_ROWS, HANDS), jnp.bfloat16),
+            pltpu.VMEM((LOCAL * OWNED, DEVICES, 128), jnp.bfloat16),
+            pltpu.VMEM((LOCAL * BOARD_ROWS, HANDS), jnp.float32),
+            pltpu.VMEM((LOCAL * BOARD_ROWS, HANDS), jnp.float32),
             pltpu.VMEM((128, 128), jnp.float32),
-            pltpu.SemaphoreType.DMA,
+            pltpu.SemaphoreType.DMA((3,)),
         ],
         compiler_params=pltpu.CompilerParams(vmem_limit_bytes=VMEM),
         name="board_values",
-    )(turn_cards, cards, recv, apart)
-
-
-def turn_kernel(recv, out, turned):
+    )(turn_cards, cards, recv, apart, marks_in, marks_out)
+
+
+def turn_kernel(recv, out, turned, best):
     group = DEVICES // TURNS
     line_sum = jnp.zeros((TURNS, 128), jnp.float32)
     for g in range(group):
@@ -489,17 +608,19 @@
         folder = TREE[leaf]["folder"]
         lost = PRE_POT + TREE[leaf]["put"][folder]
         leaf_values[leaf] = folds[:, 8 * f + 8 : 8 * f + 16] * (lost if folder == 1 else -lost)
-    out[...] = back_up(leaf_values)
+    best[0:OWNED, 0:TURNS] = back_up(leaf_values)
+    out[...] = best[...].T[0:TURNS, 0:OWNED]
 
 
 def turns(recv):
     vmem = pl.BlockSpec(memory_space=pltpu.VMEM)
+    (recv,) = keep(pltpu.VMEM, recv)
     return pl.pallas_call(
         turn_kernel,
         in_specs=[vmem],
         out_specs=vmem,
-        out_shape=jax.ShapeDtypeStruct((OWNED, TURNS), jnp.float32),
-        scratch_shapes=[pltpu.VMEM((128, 128), jnp.float32)],
+        out_shape=jax.ShapeDtypeStruct((TURNS, OWNED), jnp.float32),
+        scratch_shapes=[pltpu.VMEM((128, 128), jnp.float32), pltpu.VMEM((128, 128), jnp.float32)],
         name="turn_values",
     )(recv)
 
@@ -512,20 +633,33 @@
     cards[0], cards[1] = low, high
     deck = np.arange(128)
     marks = ((low[:, None] == deck) | (high[:, None] == deck)).astype(np.float32)
-
-    packed = send(turn_cards, cum_turn, opp_init, strength, cum_river)
+    marks_in = np.zeros((HANDS, 256), np.float32)
+    marks_out = np.zeros((256, HANDS), np.float32)
+    for copy in range(3):
+        marks_in[:, 64 * copy : 64 * copy + 64] = marks[:, 0:64]
+        marks_out[64 * copy : 64 * copy + 52] = 0.5 - marks.T[0:52]
+
+    turn_cards = turn_cards.T
+    packed = send(
+        turn_cards, jnp.transpose(cum_turn, (0, 2, 1)), opp_init.T, strength, cum_river
+    )
     packed = packed.reshape(DEVICES, BLOCKS, 128)
     recv = lax.all_to_all(packed, AXES, split_axis=0, concat_axis=0, tiled=True)
     apart = make_apart(jnp.asarray(marks, jnp.bfloat16))
     river, sums = boards(
-        turn_cards, jnp.asarray(cards), recv.reshape(DEVICES * BLOCKS, 128), apart
+        turn_cards,
+        jnp.asarray(cards),
+        recv.reshape(DEVICES * BLOCKS, 128),
+        apart,
+        jnp.asarray(marks_in, jnp.bfloat16),
+        jnp.asarray(marks_out, jnp.bfloat16),
     )
     back = lax.all_to_all(
         sums.reshape(DEVICES, 1, 128), AXES, split_axis=0, concat_axis=0, tiled=True
     )
     river = river.reshape(LOCAL, LINES, OWNED, DEVICES)
     river_value = jnp.transpose(river, (0, 1, 3, 2)).reshape(LOCAL, LINES, HANDS)
-    return river_value, turns(back.reshape(DEVICES, 128))
+    return river_value, turns(back.reshape(DEVICES, 128)).T
 
 
 def solution(mesh):

time: 72.6 us -> 57.2 us (0.79)
  local copies, waits for them, and re-layouts: 10.6 us -> 2.35 us
  Pallas kernels: 23.2 us -> 18.1 us
  waiting for transfers between devices: 22 us -> 20.2 us
    unnamed x8 -> x0, local copies, waits for them, and re-layouts: 7.24 us -> none
    pallas_call x1, Pallas kernels: 9.73 us -> 6.98 us  [boards(): pl.pallas_call(board_kernel, in_specs=[pl.BlockSpec(memory_space=pltpu.SM...]
    all_to_all x1, waiting for transfers between devices: 15.4 us -> 12.7 us  [body(): recv = lax.all_to_all(packed, AXES, split_axis=0, concat_axis=0, tiled=True)]
    pallas_call x1, Pallas kernels: 7.56 us -> 5.97 us  [send(): pl.pallas_call(send_kernel, in_specs=[pl.BlockSpec(memory_space=pltpu.SME...]
    reshape x1, local copies, waits for them, and re-layouts: 0.98 us -> 0.03 us  [body(): river = river.reshape(LOCAL, LINES, OWNED, DEVICES)]
    all_to_all x1, waiting for transfers between devices: 6.56 us -> 7.51 us  [body(): lax.all_to_all(sums.reshape(DEVICES, 1, 128), AXES, split_axis=0, concat_...]
    pallas_call x1, Pallas kernels: 1.9 us -> 1.13 us  [turns(): pl.pallas_call(turn_kernel, in_specs=[vmem], out_specs=vmem, out_shape=ja...]
  transfers between devices with their start and end apart: 2 -> 2, of which waited for: 2 -> 2; matrix products, arithmetic and copies ran while one was open for 5% -> 4% of each run, Pallas kernels for 6% -> 7%
where the time goes in v2:
time: 57.2 us; the launch traced here: 56.8 us
  waiting for transfers between devices  20.2 us (35%)
  Pallas kernels  18.1 us (32%)
  starting transfers between devices  15.4 us (27%)
  local copies, waits for them, and re-layouts  2.35 us (4%)
  between operations  0.68 us (1%)
    all_to_all x1, waiting for transfers between devices, body(): recv = lax.all_to_all(packed, AXES, split_axis=0, concat_axis=0, tiled=True)  12.7 us
    all_to_all x1, starting transfers between devices, body(): recv = lax.all_to_all(packed, AXES, split_axis=0, concat_axis=0, tiled=True)  11.5 us
    all_to_all x1, waiting for transfers between devices, body(): lax.all_to_all(sums.reshape(DEVICES, 1, 128), AXES, split_axis=0, concat_...  7.51 us
    pallas_call x1, Pallas kernels, boards(): pl.pallas_call(board_kernel, in_specs=[pl.BlockSpec(memory_space=pltpu.SM...  6.98 us
    pallas_call x1, Pallas kernels, send(): pl.pallas_call(send_kernel, in_specs=[pl.BlockSpec(memory_space=pltpu.SME...  5.97 us
    pallas_call x1, Pallas kernels, make_apart(): pl.pallas_call(apart_kernel, in_specs=[vmem], out_specs=vmem, out_shape=p...  4.07 us
    all_to_all x1, starting transfers between devices, body(): lax.all_to_all(sums.reshape(DEVICES, 1, 128), AXES, split_axis=0, concat_...  3.94 us
    reshape x1, local copies, waits for them, and re-layouts, body(): jnp.transpose(river, (0, 1, 3, 2)).reshape(LOCAL, LINES, HANDS)  1.75 us
  transfers between devices with their start and end apart: 2, of which 2 were waited for; matrix products, arithmetic and copies ran while one was open for 4% of the time, Pallas kernels for 7%

profile of v2, /device:TPU:1, one launch (start us, length us, event | category | flops | bytes accessed | tf_op | source)
XLA Modules:
  0.0 56.8 jit_solution(1715952604882654080)
XLA Ops:
  0.6 6.0 %send_reach.1 = bf16[3072,128]{1,0:T(8,128)(2,1)} custom-call(s32[4,8]{1,0:T(4,128)} %bitcast.20, f32[11,8,13]{2,1,0:T(8,128)} %bitcast.19, f32[8,11]{1,0:T(8,128)} %bitcast.22, s32[11,384]{1,0:T(8,128)} %strength.1, f32[11,9,13,384]{3,2,1,0:T(8,128)} %cum_river.1), custom_call_target="tpu_custom_call" | custom-call | tf_op jit(solution)/shard_map/send_reach/pallas_call | solution.py:337
  6.6 11.5 %all-to-all-start = ((bf16[128,24,128]{2,1,0:T(8,128)(2,1)}), bf16[128,24,128]{2,1,0:T(8,128)(2,1)S(1)}, u32[]{:S(2)}, u32[]{:S(2)}) async-start(bf16[128,24,128]{2,1,0:T(8,128)(2,1)} %bitcast.3), calls=%async_computation | async-start | bytes 1572864 | tf_op jit(solution)/shard_map/all_to_all | solution.py:647
  18.1 4.1 %apart_pairs.1.apart_hbm = bf16[1408,1408]{1,0:T(8,128)(2,1)} custom-call(bf16[1408,128]{1,0:T(8,128)(2,1)} %constant.8.clone.marks), custom_call_target="tpu_custom_call" | custom-call | tf_op jit(solution)/shard_map/apart_pairs/pallas_call | solution.py:371
  22.2 12.7 %all-to-all-done = bf16[128,24,128]{2,1,0:T(8,128)(2,1)S(1)} async-done(((bf16[128,24,128]{2,1,0:T(8,128)(2,1)}), bf16[128,24,128]{2,1,0:T(8,128)(2,1)S(1)}, u32[]{:S(2)}, u32[]{:S(2)}) %all-to-all-start) | async-done | bytes 786464 | tf_op jit(solution)/shard_map/all_to_all | solution.py:647
  34.9 7.0 %board_values.1 = (f32[3,9,1408]{2,1,0:T(8,128)S(1)}, f32[128,128]{1,0:T(8,128)}) custom-call(s32[4,8]{1,0:T(4,128)} %bitcast.21, s32[8,1408]{1,0:T(8,128)} %constant.9.clone.cards, bf16[3072,128]{1,0:T(8,128)(2,1)S(1)} %bitcast.16, bf16[1408,1408]{1,0:T(8,128)(2,1)} %apart_pairs.1.apart_hbm, bf16[1408,256]{1,0:T(8,128)(2,1)} %constant.10.clone.marks_in_hbm, ...), custom_call_target="tpu_custom_call" | custom-call | tf_op jit(solution)/shard_map/board_values/pallas_call | solution.py:563
  41.9 3.9 %all-to-all-start.1 = ((f32[128,1,128]{2,1,0:T(1,128)}), f32[128,1,128]{2,1,0:T(1,128)S(1)}, u32[]{:S(2)}, u32[]{:S(2)}) async-start(f32[128,1,128]{2,1,0:T(1,128)} %bitcast.8), calls=%async_computation.1 | async-start | bytes 131072 | tf_op jit(solution)/shard_map/all_to_all | solution.py:657
  45.9 0.6 %copy.15 = f32[3,9,128,11]{3,2,0,1:T(8,128)S(1)} copy(f32[3,9,128,11]{2,3,1,0:T(8,128)S(1)} %bitcast.18) | data formatting | bytes 304128 | tf_op jit(solution)/shard_map/transpose | solution.py:661
  46.4 1.7 %reshape.25 = f32[3,9,1408]{2,0,1:T(4,128)} reshape(f32[3,9,128,11]{3,2,0,1:T(8,128)S(1)} %copy.15) | data formatting | bytes 304128 | tf_op jit(solution)/shard_map/reshape | solution.py:661
  48.2 7.5 %all-to-all-done.1 = f32[128,1,128]{2,1,0:T(1,128)S(1)} async-done(((f32[128,1,128]{2,1,0:T(1,128)}), f32[128,1,128]{2,1,0:T(1,128)S(1)}, u32[]{:S(2)}, u32[]{:S(2)}) %all-to-all-start.1) | async-done | bytes 65568 | tf_op jit(solution)/shard_map/all_to_all | solution.py:657
  55.7 1.1 %turn_values.1 = f32[8,11]{1,0:T(8,128)} custom-call(f32[128,128]{1,0:T(8,128)S(1)} %bitcast.17), custom_call_target="tpu_custom_call" | custom-call | tf_op jit(solution)/shard_map/turn_values/pallas_call | solution.py:618
  (1 shorter events, 0.0 us)
Async XLA Ops:
  6.6 28.3 %all-to-all-start = ((bf16[128,24,128]{2,1,0:T(8,128)(2,1)}), bf16[128,24,128]{2,1,0:T(8,128)(2,1)S(1)}, u32[]{:S(2)}, u32[]{:S(2)}) async-start(bf16[128,24,128]{2,1,0:T(8,128)(2,1)} %bitcast.3), calls=%async_computation | async-start | bytes 1572864 | tf_op jit(solution)/shard_map/all_to_all | solution.py:647
  41.9 13.8 %all-to-all-start.1 = ((f32[128,1,128]{2,1,0:T(1,128)}), f32[128,1,128]{2,1,0:T(1,128)S(1)}, u32[]{:S(2)}, u32[]{:S(2)}) async-start(f32[128,1,128]{2,1,0:T(1,128)} %bitcast.8), calls=%async_computation.1 | async-start | bytes 131072 | tf_op jit(solution)/shard_map/all_to_all | solution.py:657

commit v3 on v2

--- a/solution.py
+++ b/solution.py
@@ -11,6 +11,7 @@
 BETS = 4
 PRE_POT = 2.0
 UNROLL = True
+GROUP = 3
 AXES = ("board", "hand")
 
 HANDS = 1408
@@ -24,11 +25,13 @@
 SLOTS = 88
 BOARD_SLOTS = OWNED * SLOTS
 BLOCKS = 24
-USED_BLOCKS = 23
+BOARD_BLOCKS = BLOCKS // LOCAL
+CHUNK = 256
+CHUNKS = -(-HANDS // CHUNK)
 PITCH = 24
 BOARD_ROWS = 96
 LEVEL_SLOT = 81
-VMEM = 48 * 1024 * 1024
+VMEM = 32 * 1024 * 1024
 
 
 def grow_street(bet_cap):
@@ -157,13 +160,43 @@
 
 
 def send_kernel(
-    turn_cards, cum_turn, opp_init, strength, cum_river, out, cum, turn_rows, root, reach, wide, sems
+    turn_cards_hbm,
+    cum_turn_hbm,
+    opp_init_hbm,
+    strength_hbm,
+    cum_river,
+    out,
+    turn_cards,
+    cum_turn,
+    opp_init,
+    strength,
+    cum,
+    turn_rows,
+    root,
+    reach,
+    by_board,
+    wide,
+    sems,
 ):
-    def fetch(k):
-        return pltpu.make_async_copy(cum_river.at[k], cum.at[k], sems.at[k])
-
-    for k in range(OWNED):
-        fetch(k).start()
+    loads = [
+        pltpu.make_async_copy(source, target, sems.at[i])
+        for i, (source, target) in enumerate(
+            [
+                (cum_turn_hbm, cum_turn),
+                (opp_init_hbm, opp_init),
+                (turn_cards_hbm, turn_cards),
+                (strength_hbm, strength),
+            ]
+        )
+    ]
+    fetches = []
+    for i, first in enumerate(range(0, OWNED, GROUP)):
+        part = pl.ds(first, min(GROUP, OWNED - first))
+        fetches.append(
+            pltpu.make_async_copy(cum_river.at[part], cum.at[part], sems.at[len(loads) + i])
+        )
+    for copy in loads + fetches:
+        copy.start()
     f32 = jnp.float32
     first_hand = device_index() * OWNED
     hand = first_hand + lax.broadcasted_iota(jnp.int32, (16, 1), 0)
@@ -175,6 +208,7 @@
     turn = jnp.zeros((1, BOARDS), jnp.int32)
     for q in range(1, TURNS):
         turn = turn + jnp.where(board >= RIVERS * q, 1, 0)
+    loads[2].wait()
     cards = []
     for c in range(4):
         card = jnp.zeros((1, BOARDS), jnp.int32)
@@ -189,6 +223,8 @@
     alive = jnp.where(free & (low != river) & (high != river), 1.0, 0.0).astype(f32)
 
     turn_rows[...] = jnp.zeros(turn_rows.shape, f32)
+    loads[0].wait()
+    loads[1].wait()
     turn_rows[0 : OWNED * TURNS, 0:ROWS] = cum_turn[...].reshape(OWNED * TURNS, ROWS)
     turn_rows[128 : 128 + TURNS, 0:OWNED] = opp_init[...]
     by_row = turn_rows[0:128, :].T
@@ -233,12 +269,15 @@
     folded = folded * alive_turn
     fold_head = folded.astype(jnp.bfloat16).astype(f32)
     fold_tail = folded - fold_head
+    loads[3].wait()
     level = strength[...].astype(f32)
     for k in range(OWNED):
-        reach[k, 80:88, :] = jnp.zeros((8, BOARDS), f32)
-        reach[k, 81:82, :] = level[k : k + 1]
-        reach[k, 82:83, :] = fold_head[k : k + 1]
-        reach[k, 83:84, :] = fold_tail[k : k + 1]
+        base = SLOTS * k
+        reach[base + 80 : base + 88, :] = jnp.zeros((8, BOARDS), f32)
+        reach[base + 81 : base + 82, :] = level[k : k + 1]
+        reach[base + 82 : base + 83, :] = fold_head[k : k + 1]
+        reach[base + 83 : base + 84, :] = fold_tail[k : k + 1]
+    reach[BOARD_SLOTS:, :] = jnp.zeros((128 * BOARD_BLOCKS - BOARD_SLOTS, BOARDS), f32)
 
     row_head = lax.broadcasted_iota(jnp.int32, (8, 1), 0)
     row_tail = lax.broadcasted_iota(jnp.int32, (8, 1), 0) + 8
@@ -250,8 +289,7 @@
             merged = jnp.where(row_ids <= rows[-1], part, merged)
         return merged
 
-    def one_hand(k, carry):
-        fetch(k).wait()
+    def one_hand(k):
         for line in range(LINES):
             x_head = cum[k, line, 0:8, :]
             x_tail = jnp.concatenate([cum[k, line, 8:13, :], jnp.ones((3, BOARDS), f32)], 0)
@@ -276,52 +314,25 @@
                 pltpu.roll(tail, 6, 0),
                 jnp.where(row_head == 4, pltpu.roll(tail, 4, 0), head),
             )
-            reach[k, 8 * line : 8 * line + 8, :] = mixed
-            reach[k, 72 + line : 73 + line, :] = tail[4:5]
-        return carry
-
-    lax.fori_loop(0, OWNED, one_hand, 0, unroll=True)
-
-    dest = lax.broadcasted_iota(jnp.int32, (DEVICES, BOARDS), 0)
-    lane = lax.broadcasted_iota(jnp.int32, (DEVICES, BOARDS), 1)
-    picks = [
-        jnp.where(lane == LOCAL * dest + b, 1.0, 0.0).astype(jnp.bfloat16) for b in range(LOCAL)
-    ]
-    block_lane = lax.broadcasted_iota(jnp.int32, (DEVICES, 128), 1)
-
-    def pick(b, values):
-        return lax.dot_general(
-            picks[b],
-            values.astype(jnp.bfloat16),
-            (((1,), (1,)), ((), ())),
-            preferred_element_type=f32,
-        )
-
-    flat = reach.reshape(BOARD_SLOTS, BOARDS)
-
-    def put(m, block):
-        wide.reshape(DEVICES * PITCH, 128)[pl.ds(m, DEVICES, stride=PITCH), :] = block
-
-    for b in range(LOCAL):
-        first = -(-b * BOARD_SLOTS // 128)
-        last = (b + 1) * BOARD_SLOTS // 128
-
-        def whole_block(m, carry):
-            start = pl.multiple_of(128 * m - b * BOARD_SLOTS, 8)
-            put(m, pick(b, flat[pl.ds(start, 128), :]))
-            return carry
-
-        lax.fori_loop(first, last, whole_block, 0, unroll=UNROLL)
-        inside = 128 * last - b * BOARD_SLOTS
-        room = BOARD_SLOTS - inside
-        part = flat[inside:BOARD_SLOTS, :]
-        if b == LOCAL - 1:
-            put(last, pick(b, jnp.concatenate([part, jnp.zeros((128 - room, BOARDS), f32)], 0)))
-        else:
-            both = jnp.concatenate([part, flat[0 : 128 - room, :]], 0)
-            put(last, jnp.where(block_lane < room, pick(b, both), pick(b + 1, both)))
-    for m in range(USED_BLOCKS, BLOCKS):
-        put(m, jnp.zeros((DEVICES, 128), f32))
+            base = SLOTS * k
+            reach[base + 8 * line : base + 8 * line + 8, :] = mixed
+            reach[base + 72 + line : base + 73 + line, :] = tail[4:5]
+
+    for k in range(OWNED):
+        if k % GROUP == 0:
+            fetches[k // GROUP].wait()
+        one_hand(k)
+
+    flat_wide = wide.reshape(DEVICES * PITCH, 128)
+    for j in range(BOARD_BLOCKS):
+        for i in range(LOCAL):
+            by_board[j, 128 * i : 128 * i + 128, :] = reach[
+                128 * j : 128 * j + 128, 128 * i : 128 * i + 128
+            ].T
+        for b in range(LOCAL):
+            flat_wide[pl.ds(BOARD_BLOCKS * b + j, DEVICES, stride=PITCH), :] = by_board[
+                j, pl.ds(b, DEVICES, stride=LOCAL), :
+            ]
     out[...] = wide[:, 0:BLOCKS, :].astype(jnp.bfloat16).reshape(DEVICES * BLOCKS, 128)
 
 
@@ -330,52 +341,28 @@
 
 
 def send(turn_cards, cum_turn, opp_init, strength, cum_river):
-    vmem = pl.BlockSpec(memory_space=pltpu.VMEM)
-    turn_cards, cum_turn, opp_init, strength, cum_river = keep(
-        pltpu.HBM, turn_cards, cum_turn, opp_init, strength, cum_river
-    )
+    args = keep(pltpu.HBM, turn_cards, cum_turn, opp_init, strength, cum_river)
     return pl.pallas_call(
         send_kernel,
-        in_specs=[
-            pl.BlockSpec(memory_space=pltpu.SMEM),
-            vmem,
-            vmem,
-            vmem,
-            pl.BlockSpec(memory_space=pl.ANY),
-        ],
-        out_specs=vmem,
+        in_specs=[pl.BlockSpec(memory_space=pl.ANY)] * len(args),
+        out_specs=pl.BlockSpec(memory_space=pltpu.VMEM),
         out_shape=pltpu.VMEM((DEVICES * BLOCKS, 128), jnp.bfloat16),
         scratch_shapes=[
+            pltpu.SMEM(turn_cards.shape, jnp.int32),
+            pltpu.VMEM(cum_turn.shape, jnp.float32),
+            pltpu.VMEM(opp_init.shape, jnp.float32),
+            pltpu.VMEM(strength.shape, jnp.int32),
             pltpu.VMEM((OWNED, LINES, ROWS, BOARDS), jnp.float32),
             pltpu.VMEM((256, 128), jnp.float32),
             pltpu.VMEM((LINES, 16, BOARDS), jnp.float32),
-            pltpu.VMEM((OWNED, SLOTS, BOARDS), jnp.float32),
+            pltpu.VMEM((128 * BOARD_BLOCKS, BOARDS), jnp.float32),
+            pltpu.VMEM((BOARD_BLOCKS, BOARDS, 128), jnp.float32),
             pltpu.VMEM((DEVICES, PITCH, 128), jnp.float32),
-            pltpu.SemaphoreType.DMA((OWNED,)),
+            pltpu.SemaphoreType.DMA((4 + -(-OWNED // GROUP),)),
         ],
         compiler_params=pltpu.CompilerParams(vmem_limit_bytes=VMEM),
         name="send_reach",
-    )(turn_cards, cum_turn, opp_init, strength, cum_river)
-
-
-def apart_kernel(marks, out):
-    shared = lax.dot_general(
-        marks[...], marks[...], (((1,), (1,)), ((), ())), preferred_element_type=jnp.float32
-    )
-    out[...] = jnp.where(shared == 0.0, 1.0, 0.0).astype(jnp.bfloat16)
-
-
-def make_apart(marks):
-    vmem = pl.BlockSpec(memory_space=pltpu.VMEM)
-    (marks,) = keep(pltpu.HBM, marks)
-    return pl.pallas_call(
-        apart_kernel,
-        in_specs=[vmem],
-        out_specs=vmem,
-        out_shape=pltpu.HBM((HANDS, HANDS), jnp.bfloat16),
-        compiler_params=pltpu.CompilerParams(vmem_limit_bytes=VMEM),
-        name="apart_pairs",
-    )(marks)
+    )(*args)
 
 
 def stake_column(rows):
@@ -412,17 +399,13 @@
 
 
 def board_kernel(
-    turn_cards,
+    turn_cards_hbm,
     cards,
     recv,
-    apart_hbm,
-    marks_in_hbm,
-    marks_out_hbm,
+    pairs,
     river_out,
     sums_out,
-    apart,
-    marks_in,
-    marks_out,
+    turn_cards,
     wide,
     turned,
     lhs,
@@ -434,41 +417,45 @@
 ):
     f32 = jnp.float32
     bf16 = jnp.bfloat16
-    loads = [
-        pltpu.make_async_copy(marks_in_hbm, marks_in, sems.at[0]),
-        pltpu.make_async_copy(marks_out_hbm, marks_out, sems.at[1]),
-        pltpu.make_async_copy(apart_hbm, apart, sems.at[2]),
-    ]
-    for load in loads:
-        load.start()
+    card_load = pltpu.make_async_copy(turn_cards_hbm, turn_cards, sems.at[0])
+    card_load.start()
     wide[:, 0:BLOCKS, :] = recv[...].astype(f32).reshape(DEVICES, BLOCKS, 128)
-
-    def turn_block(m, carry):
+    for m in range(BLOCKS):
         block = wide.reshape(DEVICES * PITCH, 128)[pl.ds(m, DEVICES, stride=PITCH), :]
-        turned[pl.ds(pl.multiple_of(128 * m, 128), 128), :] = block.T
-        return carry
-
-    lax.fori_loop(0, USED_BLOCKS, turn_block, 0, unroll=UNROLL)
-
+        turned[128 * m : 128 * m + 128, :] = block.T
     for b in range(LOCAL):
-
-        def one_hand(k, carry):
-            base = pl.multiple_of(SLOTS * (OWNED * b + k), 8)
-            lanes = pl.ds(pl.multiple_of(128 * k, 128), 128)
+        for k in range(OWNED):
+            base = 128 * BOARD_BLOCKS * b + SLOTS * k
             parts = [turned[pl.ds(base + g, 8, stride=8), :] for g in range(8)]
             for first in (72, 64, 80):
                 parts.append(turned[pl.ds(base + first, 8), :])
             parts.append(jnp.zeros((8, 128), f32))
-            lhs[BOARD_ROWS * b : BOARD_ROWS * (b + 1), lanes] = jnp.concatenate(parts, 0).astype(
-                bf16
-            )
-            return carry
-
-        lax.fori_loop(0, OWNED, one_hand, 0, unroll=UNROLL)
-
+            lhs[BOARD_ROWS * b : BOARD_ROWS * (b + 1), 128 * k : 128 * k + 128] = jnp.concatenate(
+                parts, 0
+            ).astype(bf16)
+
+    def fold_sums(rows):
+        card_marks = pairs[HANDS : HANDS + 256, :]
+        card_sums = lax.dot_general(
+            lhs[rows, :], card_marks, (((1,), (1,)), ((), ())), preferred_element_type=f32
+        )
+        others = card_sums[:, 52:53] - card_sums
+        lane = lax.broadcasted_iota(jnp.int32, others.shape, 1)
+        head = others.astype(bf16).astype(f32)
+        middle = (others - head).astype(bf16).astype(f32)
+        tail = others - head - middle
+        split = jnp.where(lane < 64, head, jnp.where(lane < 128, middle, tail)).astype(bf16)
+        folds[rows, :] = jnp.dot(split, card_marks, preferred_element_type=f32) + lhs[
+            rows, :
+        ].astype(f32)
+
+    fold_sums(slice(0, LOCAL * BOARD_ROWS))
     level_rows = jnp.concatenate(
         [
-            turned[pl.ds(LEVEL_SLOT, LOCAL * OWNED, stride=SLOTS), :],
+            turned[pl.ds(128 * BOARD_BLOCKS * b + LEVEL_SLOT, OWNED, stride=SLOTS), :]
+            for b in range(LOCAL)
+        ]
+        + [
             jnp.zeros((128 - LOCAL * OWNED, 128), f32),
         ],
         0,
@@ -478,16 +465,7 @@
         column = level_columns[:, q : q + 1]
         columns[q] = jnp.broadcast_to(column, (DEVICES, 128)).astype(bf16)
 
-    loads[0].wait()
-    loads[1].wait()
-    card_sums = jnp.dot(lhs[...], marks_in[...], preferred_element_type=f32)
-    lane = lax.broadcasted_iota(jnp.int32, card_sums.shape, 1)
-    head = card_sums.astype(bf16).astype(f32)
-    middle = (card_sums - head).astype(bf16).astype(f32)
-    tail = card_sums - head - middle
-    split = jnp.where(lane < 64, head, jnp.where(lane < 128, middle, tail)).astype(bf16)
-    folds[...] = jnp.dot(split, marks_out[...], preferred_element_type=f32) + lhs[...].astype(f32)
-    loads[2].wait()
+    card_load.wait()
 
     first_board = device_index() * LOCAL
     turn = first_board // RIVERS
@@ -500,78 +478,76 @@
     alive_turn = jnp.where(free, 1.0, 0.0).astype(f32)
     stake = stake_column(8)
     last_stake = PRE_POT + LINE_PUT[8]
-    total = jnp.zeros((8, HANDS), f32)
-    last_total = jnp.zeros((1, HANDS), f32)
+    alive = []
+    level_tiles = []
     for b in range(LOCAL):
         river = river_from(board_cards, first_board + b - turn * RIVERS)
-        alive = jnp.where(free & (low != river) & (high != river), 1.0, 0.0).astype(f32)
-        row_tiles = [
-            jnp.concatenate(
-                [jnp.broadcast_to(level_rows[OWNED * b + k : OWNED * b + k + 1], (16, 128))] * 8, 0
-            ).astype(bf16)
-            for k in range(OWNED)
-        ]
-        rows = slice(BOARD_ROWS * b, BOARD_ROWS * (b + 1))
-        for first in range(0, OWNED, 2):
-            tiles = range(first, min(first + 2, OWNED))
-            lanes = slice(128 * first, 128 * (tiles[-1] + 1))
+        alive.append(jnp.where(free & (low != river) & (high != river), 1.0, 0.0).astype(f32))
+        level_tiles.append(
+            [
+                jnp.concatenate(
+                    [jnp.broadcast_to(level_rows[OWNED * b + k : OWNED * b + k + 1], (16, 128))] * 8,
+                    0,
+                ).astype(bf16)
+                for k in range(OWNED)
+            ]
+        )
+    marks[...] = jnp.zeros((128, 128), f32)
+    for b in range(LOCAL):
+        base = BOARD_ROWS * b
+        for n in range(CHUNKS):
+            tiles = range(2 * n, min(2 * n + 2, OWNED))
+            lanes = slice(CHUNK * n, CHUNK * n + 128 * len(tiles))
             signs = []
             for k in range(OWNED):
                 column = columns[OWNED * b + k]
                 pieces = []
-                for i in tiles:
-                    pair = apart[128 * k : 128 * k + 128, 128 * i : 128 * i + 128]
-                    pieces.append(jnp.clip(row_tiles[i] - column, -1.0, 1.0) * pair)
+                for tile in tiles:
+                    pair = pairs[128 * k : 128 * k + 128, 128 * tile : 128 * tile + 128]
+                    pieces.append(jnp.clip(level_tiles[b][tile] - column, -1.0, 1.0) * pair)
                 signs.append(jnp.concatenate(pieces, 1))
-            sign = jnp.concatenate(signs, 0)
-            ends[rows, lanes] = jnp.dot(lhs[rows, :], sign, preferred_element_type=f32)
-        base = BOARD_ROWS * b
+            ends[base : base + BOARD_ROWS, lanes] = jnp.dot(
+                lhs[base : base + BOARD_ROWS, :],
+                jnp.concatenate(signs, 0),
+                preferred_element_type=f32,
+            )
 
         def main_rows(sums):
-            return {
-                r: sums[base + 8 * i : base + 8 * i + 8, :] for i, r in enumerate(SENT)
-            }
+            return {r: sums[base + 8 * i : base + 8 * i + 8, :] for i, r in enumerate(SENT)}
 
         def last_rows(sums):
             return {r: sums[base + 72 + i : base + 73 + i, :] for i, r in enumerate(SENT)}
 
-        values = street_values(stake, main_rows(ends), main_rows(folds))
-        last = street_values(last_stake, last_rows(ends), last_rows(folds))
-        values = values * alive
-        last = last * alive
+        values = street_values(stake, main_rows(ends), main_rows(folds)) * alive[b]
+        last = street_values(last_stake, last_rows(ends), last_rows(folds)) * alive[b]
         river_out[b, 0:8, :] = values
         river_out[b, 8:9, :] = last
-        total = total + values
-        last_total = last_total + last
+        total = values if b == 0 else total + values
+        last_total = last if b == 0 else last_total + last
     fold_total = (folds[82:83, :] + folds[83:84, :]) * alive_turn
-    marks[...] = jnp.zeros((128, 128), f32)
     for k in range(OWNED):
         lanes = slice(128 * k, 128 * k + 128)
-        marks[8 * k : 8 * k + 8, :] = total[:, lanes]
+        marks[pl.ds(k, 8, stride=OWNED), :] = total[:, lanes]
         marks[88 + k : 89 + k, :] = last_total[:, lanes]
         marks[99 + k : 100 + k, :] = fold_total[:, lanes]
     sums_out[...] = marks[...].T
 
 
-def boards(turn_cards, cards, recv, apart, marks_in, marks_out):
+def boards(turn_cards, cards, recv, pairs):
     vmem = pl.BlockSpec(memory_space=pltpu.VMEM)
     hbm = pl.BlockSpec(memory_space=pl.ANY)
-    (recv,) = keep(pltpu.VMEM, recv)
-    turn_cards, cards, apart, marks_in, marks_out = keep(
-        pltpu.HBM, turn_cards, cards, apart, marks_in, marks_out
-    )
+    recv, cards, pairs = keep(pltpu.VMEM, recv, cards, pairs)
+    (turn_cards,) = keep(pltpu.HBM, turn_cards)
     return pl.pallas_call(
         board_kernel,
-        in_specs=[pl.BlockSpec(memory_space=pltpu.SMEM), vmem, vmem, hbm, hbm, hbm],
+        in_specs=[hbm, vmem, vmem, vmem],
         out_specs=(vmem, vmem),
         out_shape=(
             jax.ShapeDtypeStruct((LOCAL, LINES, HANDS), jnp.float32),
             pltpu.VMEM((DEVICES, 128), jnp.float32),
         ),
         scratch_shapes=[
-            pltpu.VMEM((HANDS, HANDS), jnp.bfloat16),
-            pltpu.VMEM((HANDS, 256), jnp.bfloat16),
-            pltpu.VMEM((256, HANDS), jnp.bfloat16),
+            pltpu.SMEM(turn_cards.shape, jnp.int32),
             pltpu.VMEM((DEVICES, PITCH, 128), jnp.float32),
             pltpu.VMEM((DEVICES * BLOCKS, 128), jnp.float32),
             pltpu.VMEM((LOCAL * BOARD_ROWS, HANDS), jnp.bfloat16),
@@ -579,37 +555,28 @@
             pltpu.VMEM((LOCAL * BOARD_ROWS, HANDS), jnp.float32),
             pltpu.VMEM((LOCAL * BOARD_ROWS, HANDS), jnp.float32),
             pltpu.VMEM((128, 128), jnp.float32),
-            pltpu.SemaphoreType.DMA((3,)),
+            pltpu.SemaphoreType.DMA((1,)),
         ],
         compiler_params=pltpu.CompilerParams(vmem_limit_bytes=VMEM),
         name="board_values",
-    )(turn_cards, cards, recv, apart, marks_in, marks_out)
-
-
-def turn_kernel(recv, out, turned, best):
+    )(turn_cards, cards, recv, pairs)
+
+
+def turn_kernel(recv, out):
     group = DEVICES // TURNS
-    line_sum = jnp.zeros((TURNS, 128), jnp.float32)
-    for g in range(group):
+    line_sum = recv[pl.ds(0, TURNS, stride=group), :]
+    for g in range(1, group):
         line_sum = line_sum + recv[pl.ds(g, TURNS, stride=group), :]
-    parts = [line_sum]
-    for f in range(len(FOLDS)):
-        parts.append(recv[pl.ds(f, TURNS, stride=group), :])
-    parts.append(jnp.zeros((128 - 8 * len(parts), 128), jnp.float32))
-    turned[...] = jnp.concatenate(parts, 0).T
+    line_sum = line_sum / float(RIVERS)
     leaf_values = {}
     for line, leaf in enumerate(ENDS):
-        if line < 8:
-            value = turned[pl.ds(line, OWNED, stride=8), :]
-        else:
-            value = turned[88 : 88 + OWNED, :]
-        leaf_values[leaf] = value[:, 0:TURNS] / float(RIVERS)
-    folds = turned[99 : 99 + OWNED, :]
+        leaf_values[leaf] = pltpu.roll(line_sum, (128 - OWNED * line) % 128, 1)
     for f, leaf in enumerate(FOLDS):
         folder = TREE[leaf]["folder"]
         lost = PRE_POT + TREE[leaf]["put"][folder]
-        leaf_values[leaf] = folds[:, 8 * f + 8 : 8 * f + 16] * (lost if folder == 1 else -lost)
-    best[0:OWNED, 0:TURNS] = back_up(leaf_values)
-    out[...] = best[...].T[0:TURNS, 0:OWNED]
+        fold = pltpu.roll(recv[pl.ds(f, TURNS, stride=group), :], 128 - OWNED * LINES, 1)
+        leaf_values[leaf] = fold * (lost if folder == 1 else -lost)
+    out[...] = back_up(leaf_values)[:, 0:OWNED]
 
 
 def turns(recv):
@@ -620,7 +587,6 @@
         in_specs=[vmem],
         out_specs=vmem,
         out_shape=jax.ShapeDtypeStruct((TURNS, OWNED), jnp.float32),
-        scratch_shapes=[pltpu.VMEM((128, 128), jnp.float32), pltpu.VMEM((128, 128), jnp.float32)],
         name="turn_values",
     )(recv)
 
@@ -633,11 +599,12 @@
     cards[0], cards[1] = low, high
     deck = np.arange(128)
     marks = ((low[:, None] == deck) | (high[:, None] == deck)).astype(np.float32)
-    marks_in = np.zeros((HANDS, 256), np.float32)
-    marks_out = np.zeros((256, HANDS), np.float32)
+    pairs = np.zeros((HANDS + 256, HANDS), np.float32)
+    pairs[0:HANDS] = marks @ marks.T == 0
     for copy in range(3):
-        marks_in[:, 64 * copy : 64 * copy + 64] = marks[:, 0:64]
-        marks_out[64 * copy : 64 * copy + 52] = 0.5 - marks.T[0:52]
+        first = HANDS + 64 * copy
+        pairs[first : first + 52] = marks.T[0:52]
+        pairs[first + 52] = 0.5
 
     turn_cards = turn_cards.T
     packed = send(
@@ -645,14 +612,11 @@
     )
     packed = packed.reshape(DEVICES, BLOCKS, 128)
     recv = lax.all_to_all(packed, AXES, split_axis=0, concat_axis=0, tiled=True)
-    apart = make_apart(jnp.asarray(marks, jnp.bfloat16))
     river, sums = boards(
         turn_cards,
         jnp.asarray(cards),
         recv.reshape(DEVICES * BLOCKS, 128),
-        apart,
-        jnp.asarray(marks_in, jnp.bfloat16),
-        jnp.asarray(marks_out, jnp.bfloat16),
+        jnp.asarray(pairs, jnp.bfloat16),
     )
     back = lax.all_to_all(
         sums.reshape(DEVICES, 1, 128), AXES, split_axis=0, concat_axis=0, tiled=True

time: 57.2 us -> 52.3 us (0.914)
  blocking collectives: 0 us -> 28.1 us
  waiting for transfers between devices: 20.2 us -> 7.51 us
  starting transfers between devices: 15.4 us -> 3.93 us
  Pallas kernels: 18.1 us -> 9.57 us
    all_to_all x0 -> x1, blocking collectives: none -> 28.1 us  [body(): recv = lax.all_to_all(packed, AXES, split_axis=0, concat_axis=0, tiled=True)]
    all_to_all x1 -> x0, waiting for transfers between devices: 12.7 us -> none  [body(): recv = lax.all_to_all(packed, AXES, split_axis=0, concat_axis=0, tiled=True)]
    all_to_all x1 -> x0, starting transfers between devices: 11.5 us -> none  [body(): recv = lax.all_to_all(packed, AXES, split_axis=0, concat_axis=0, tiled=True)]
    pallas_call x3 -> x2, Pallas kernels: 17 us -> 8.87 us  [the longest x1 5.1 us: boards(): pl.pallas_call(board_kernel, in_specs=[hbm, vmem, vmem, vmem], out_specs=...]
  transfers between devices with their start and end apart: 2 -> 1, of which waited for: 2 -> 1; matrix products, arithmetic and copies ran while one was open for 4% -> 5% of each run, Pallas kernels for 7% -> 0%
where the time goes in v3:
time: 52.3 us; the launch traced here: 52.1 us
  blocking collectives  28.1 us (54%)
  Pallas kernels  9.57 us (18%)
  waiting for transfers between devices  7.51 us (14%)
  starting transfers between devices  3.93 us (8%)
  local copies, waits for them, and re-layouts  2.37 us (5%)
  between operations  0.69 us (1%)
    all_to_all x1, blocking collectives, body(): recv = lax.all_to_all(packed, AXES, split_axis=0, concat_axis=0, tiled=True)  28.1 us
    all_to_all x1, waiting for transfers between devices, body(): lax.all_to_all(sums.reshape(DEVICES, 1, 128), AXES, split_axis=0, concat_...  7.51 us
    pallas_call x1, Pallas kernels, boards(): pl.pallas_call(board_kernel, in_specs=[hbm, vmem, vmem, vmem], out_specs=...  5.1 us
    all_to_all x1, starting transfers between devices, body(): lax.all_to_all(sums.reshape(DEVICES, 1, 128), AXES, split_axis=0, concat_...  3.93 us
    pallas_call x1, Pallas kernels, send(): pl.pallas_call(send_kernel, in_specs=[pl.BlockSpec(memory_space=pl.ANY)]...  3.77 us
    reshape x1, local copies, waits for them, and re-layouts, body(): jnp.transpose(river, (0, 1, 3, 2)).reshape(LOCAL, LINES, HANDS)  1.75 us
  transfers between devices with their start and end apart: 1, of which 1 were waited for; matrix products, arithmetic and copies ran while one was open for 5% of the time, Pallas kernels for 0%

profile of v3, /device:TPU:1, one launch (start us, length us, event | category | flops | bytes accessed | tf_op | source)
XLA Modules:
  0.0 52.1 jit_solution(1582372395063103689)
XLA Ops:
  0.6 0.0 copy-start
  0.6 0.0 copy-start.1
  0.7 3.8 %send_reach.1 = bf16[3072,128]{1,0:T(8,128)(2,1)S(1)} custom-call(s32[4,8]{1,0:T(4,128)} %bitcast.21, f32[11,8,13]{2,1,0:T(8,128)} %bitcast.20, f32[8,11]{1,0:T(8,128)} %bitcast.23, s32[11,384]{1,0:T(8,128)} %strength_hbm.1, f32[11,9,13,384]{3,2,1,0:T(8,128)} %cum_river.1), custom_call_target="tpu_custom_call" | custom-call | tf_op jit(solution)/shard_map/send_reach/pallas_call | solution.py:345
  4.4 28.1 %all_to_all.10 = bf16[128,24,128]{2,1,0:T(8,128)(2,1)S(1)} all-to-all(bf16[128,24,128]{2,1,0:T(8,128)(2,1)S(1)} %bitcast.16), channel_id=1, replica_groups=mesh['board'=16,'hand'=8] {'board','hand'}, dimensions={0} | all-to-all | bytes 1572864 | tf_op jit(solution)/shard_map/all_to_all | solution.py:614
  32.5 0.0 copy-done
  32.5 0.0 copy-done.1
  32.5 5.1 %board_values.1 = (f32[3,9,1408]{2,1,0:T(8,128)S(1)}, f32[128,128]{1,0:T(8,128)}) custom-call(s32[4,8]{1,0:T(4,128)} %bitcast.22, s32[8,1408]{1,0:T(8,128)S(1)} %copy-done.1, bf16[3072,128]{1,0:T(8,128)(2,1)S(1)} %bitcast.17, bf16[1664,1408]{1,0:T(8,128)(2,1)S(1)} %copy-done), custom_call_target="tpu_custom_call" | custom-call | tf_op jit(solution)/shard_map/board_values/pallas_call | solution.py:541
  37.6 3.9 %all-to-all-start.1 = ((f32[128,1,128]{2,1,0:T(1,128)}), f32[128,1,128]{2,1,0:T(1,128)S(1)}, u32[]{:S(2)}, u32[]{:S(2)}) async-start(f32[128,1,128]{2,1,0:T(1,128)} %bitcast.8), calls=%async_computation.1 | async-start | bytes 131072 | tf_op jit(solution)/shard_map/all_to_all | solution.py:621
  41.6 0.6 %copy.13 = f32[3,9,128,11]{3,2,0,1:T(8,128)S(1)} copy(f32[3,9,128,11]{2,3,1,0:T(8,128)S(1)} %bitcast.19) | data formatting | bytes 304128 | tf_op jit(solution)/shard_map/transpose | solution.py:625
  42.2 1.7 %reshape.25 = f32[3,9,1408]{2,0,1:T(4,128)} reshape(f32[3,9,128,11]{3,2,0,1:T(8,128)S(1)} %copy.13) | data formatting | bytes 304128 | tf_op jit(solution)/shard_map/reshape | solution.py:625
  43.9 7.5 %all-to-all-done.1 = f32[128,1,128]{2,1,0:T(1,128)S(1)} async-done(((f32[128,1,128]{2,1,0:T(1,128)}), f32[128,1,128]{2,1,0:T(1,128)S(1)}, u32[]{:S(2)}, u32[]{:S(2)}) %all-to-all-start.1) | async-done | bytes 65568 | tf_op jit(solution)/shard_map/all_to_all | solution.py:621
  51.4 0.7 %turn_values.1 = f32[8,11]{1,0:T(8,128)} custom-call(f32[128,128]{1,0:T(8,128)S(1)} %bitcast.18), custom_call_target="tpu_custom_call" | custom-call | tf_op jit(solution)/shard_map/turn_values/pallas_call | solution.py:585
  (1 shorter events, 0.0 us)
Async XLA Ops:
  0.6 31.9 %copy-start = (bf16[1664,1408]{1,0:T(8,128)(2,1)S(1)}, bf16[1664,1408]{1,0:T(8,128)(2,1)}, u32[]{:S(2)}) copy-start(bf16[1664,1408]{1,0:T(8,128)(2,1)} %constant.5.clone.pairs) | copy-start | bytes 14057476
  0.6 31.9 %copy-start.1 = (s32[8,1408]{1,0:T(8,128)S(1)}, s32[8,1408]{1,0:T(8,128)}, u32[]{:S(2)}) copy-start(s32[8,1408]{1,0:T(8,128)} %constant.4.clone.cards) | copy-start | bytes 135172
  37.6 13.8 %all-to-all-start.1 = ((f32[128,1,128]{2,1,0:T(1,128)}), f32[128,1,128]{2,1,0:T(1,128)S(1)}, u32[]{:S(2)}, u32[]{:S(2)}) async-start(f32[128,1,128]{2,1,0:T(1,128)} %bitcast.8), calls=%async_computation.1 | async-start | bytes 131072 | tf_op jit(solution)/shard_map/all_to_all | solution.py:621

commit v4 on v3

--- a/solution.py
+++ b/solution.py
@@ -22,15 +22,15 @@
 BOARDS = 384
 TURNS = 8
 LOCAL = BOARDS // DEVICES
-SLOTS = 88
+SLOTS = 80
 BOARD_SLOTS = OWNED * SLOTS
-BLOCKS = 24
-BOARD_BLOCKS = BLOCKS // LOCAL
+BOARD_BLOCKS = 7
+BLOCKS = LOCAL * BOARD_BLOCKS + 1
+EXTRA = LOCAL * BOARD_BLOCKS
 CHUNK = 256
 CHUNKS = -(-HANDS // CHUNK)
-PITCH = 24
+PITCH = BLOCKS
 BOARD_ROWS = 96
-LEVEL_SLOT = 81
 VMEM = 32 * 1024 * 1024
 
 
@@ -165,7 +165,9 @@
     opp_init_hbm,
     strength_hbm,
     cum_river,
+    pairs_hbm,
     out,
+    pairs,
     turn_cards,
     cum_turn,
     opp_init,
@@ -174,6 +176,7 @@
     turn_rows,
     root,
     reach,
+    rest,
     by_board,
     wide,
     sems,
@@ -195,7 +198,8 @@
         fetches.append(
             pltpu.make_async_copy(cum_river.at[part], cum.at[part], sems.at[len(loads) + i])
         )
-    for copy in loads + fetches:
+    pairs_load = pltpu.make_async_copy(pairs_hbm, pairs, sems.at[len(loads) + len(fetches)])
+    for copy in loads + fetches + [pairs_load]:
         copy.start()
     f32 = jnp.float32
     first_hand = device_index() * OWNED
@@ -271,12 +275,10 @@
     fold_tail = folded - fold_head
     loads[3].wait()
     level = strength[...].astype(f32)
-    for k in range(OWNED):
-        base = SLOTS * k
-        reach[base + 80 : base + 88, :] = jnp.zeros((8, BOARDS), f32)
-        reach[base + 81 : base + 82, :] = level[k : k + 1]
-        reach[base + 82 : base + 83, :] = fold_head[k : k + 1]
-        reach[base + 83 : base + 84, :] = fold_tail[k : k + 1]
+    rest[...] = jnp.zeros((128, BOARDS), f32)
+    rest[0:OWNED, :] = level
+    rest[OWNED : 2 * OWNED, :] = fold_head[0:OWNED]
+    rest[2 * OWNED : 3 * OWNED, :] = fold_tail[0:OWNED]
     reach[BOARD_SLOTS:, :] = jnp.zeros((128 * BOARD_BLOCKS - BOARD_SLOTS, BOARDS), f32)
 
     row_head = lax.broadcasted_iota(jnp.int32, (8, 1), 0)
@@ -316,37 +318,50 @@
             )
             base = SLOTS * k
             reach[base + 8 * line : base + 8 * line + 8, :] = mixed
-            reach[base + 72 + line : base + 73 + line, :] = tail[4:5]
+            last = base + 72 + line if line < 8 else BOARD_SLOTS + k
+            reach[last : last + 1, :] = tail[4:5]
 
     for k in range(OWNED):
         if k % GROUP == 0:
             fetches[k // GROUP].wait()
         one_hand(k)
 
-    flat_wide = wide.reshape(DEVICES * PITCH, 128)
     for j in range(BOARD_BLOCKS):
         for i in range(LOCAL):
             by_board[j, 128 * i : 128 * i + 128, :] = reach[
                 128 * j : 128 * j + 128, 128 * i : 128 * i + 128
             ].T
         for b in range(LOCAL):
-            flat_wide[pl.ds(BOARD_BLOCKS * b + j, DEVICES, stride=PITCH), :] = by_board[
+            wide[pl.ds(BOARD_BLOCKS * b + j, DEVICES, stride=PITCH), :] = by_board[
                 j, pl.ds(b, DEVICES, stride=LOCAL), :
             ]
-    out[...] = wide[:, 0:BLOCKS, :].astype(jnp.bfloat16).reshape(DEVICES * BLOCKS, 128)
+    for i in range(LOCAL):
+        by_board[BOARD_BLOCKS, 128 * i : 128 * i + 128, :] = rest[:, 128 * i : 128 * i + 128].T
+    block = by_board[BOARD_BLOCKS, pl.ds(0, DEVICES, stride=LOCAL), :]
+    for b in range(1, LOCAL):
+        block = block + pltpu.roll(
+            by_board[BOARD_BLOCKS, pl.ds(b, DEVICES, stride=LOCAL), :], 3 * OWNED * b, 1
+        )
+    wide[pl.ds(EXTRA, DEVICES, stride=PITCH), :] = block
+    out[...] = wide[...].astype(jnp.bfloat16)
+    pairs_load.wait()
 
 
 def keep(space, *arrays):
     return [pltpu.with_memory_space_constraint(array, space) for array in arrays]
 
 
-def send(turn_cards, cum_turn, opp_init, strength, cum_river):
-    args = keep(pltpu.HBM, turn_cards, cum_turn, opp_init, strength, cum_river)
+def send(turn_cards, cum_turn, opp_init, strength, cum_river, pairs):
+    args = keep(pltpu.HBM, turn_cards, cum_turn, opp_init, strength, cum_river, pairs)
+    vmem = pl.BlockSpec(memory_space=pltpu.VMEM)
     return pl.pallas_call(
         send_kernel,
         in_specs=[pl.BlockSpec(memory_space=pl.ANY)] * len(args),
-        out_specs=pl.BlockSpec(memory_space=pltpu.VMEM),
-        out_shape=pltpu.VMEM((DEVICES * BLOCKS, 128), jnp.bfloat16),
+        out_specs=(vmem, vmem),
+        out_shape=(
+            pltpu.VMEM((DEVICES * BLOCKS, 128), jnp.bfloat16),
+            pltpu.VMEM(pairs.shape, jnp.bfloat16),
+        ),
         scratch_shapes=[
             pltpu.SMEM(turn_cards.shape, jnp.int32),
             pltpu.VMEM(cum_turn.shape, jnp.float32),
@@ -356,9 +371,10 @@
             pltpu.VMEM((256, 128), jnp.float32),
             pltpu.VMEM((LINES, 16, BOARDS), jnp.float32),
             pltpu.VMEM((128 * BOARD_BLOCKS, BOARDS), jnp.float32),
-            pltpu.VMEM((BOARD_BLOCKS, BOARDS, 128), jnp.float32),
-            pltpu.VMEM((DEVICES, PITCH, 128), jnp.float32),
-            pltpu.SemaphoreType.DMA((4 + -(-OWNED // GROUP),)),
+            pltpu.VMEM((128, BOARDS), jnp.float32),
+            pltpu.VMEM((BOARD_BLOCKS + 1, BOARDS, 128), jnp.float32),
+            pltpu.VMEM((DEVICES * PITCH, 128), jnp.float32),
+            pltpu.SemaphoreType.DMA((5 + -(-OWNED // GROUP),)),
         ],
         compiler_params=pltpu.CompilerParams(vmem_limit_bytes=VMEM),
         name="send_reach",
@@ -419,17 +435,22 @@
     bf16 = jnp.bfloat16
     card_load = pltpu.make_async_copy(turn_cards_hbm, turn_cards, sems.at[0])
     card_load.start()
-    wide[:, 0:BLOCKS, :] = recv[...].astype(f32).reshape(DEVICES, BLOCKS, 128)
+    wide[...] = recv[...].astype(f32)
     for m in range(BLOCKS):
-        block = wide.reshape(DEVICES * PITCH, 128)[pl.ds(m, DEVICES, stride=PITCH), :]
+        block = wide[pl.ds(m, DEVICES, stride=PITCH), :]
         turned[128 * m : 128 * m + 128, :] = block.T
     for b in range(LOCAL):
         for k in range(OWNED):
             base = 128 * BOARD_BLOCKS * b + SLOTS * k
             parts = [turned[pl.ds(base + g, 8, stride=8), :] for g in range(8)]
-            for first in (72, 64, 80):
-                parts.append(turned[pl.ds(base + first, 8), :])
-            parts.append(jnp.zeros((8, 128), f32))
+            parts.append(turned[base + 72 : base + 80, :])
+            parts.append(turned[base + 64 : base + 72, :])
+            last = 128 * BOARD_BLOCKS * b + BOARD_SLOTS + k
+            parts.append(turned[last : last + 1, :])
+            for i in (1, 2):
+                extra = 128 * EXTRA + OWNED * i + k
+                parts.append(turned[extra : extra + 1, :])
+            parts.append(jnp.zeros((13, 128), f32))
             lhs[BOARD_ROWS * b : BOARD_ROWS * (b + 1), 128 * k : 128 * k + 128] = jnp.concatenate(
                 parts, 0
             ).astype(bf16)
@@ -450,19 +471,14 @@
         ].astype(f32)
 
     fold_sums(slice(0, LOCAL * BOARD_ROWS))
-    level_rows = jnp.concatenate(
-        [
-            turned[pl.ds(128 * BOARD_BLOCKS * b + LEVEL_SLOT, OWNED, stride=SLOTS), :]
-            for b in range(LOCAL)
-        ]
-        + [
-            jnp.zeros((128 - LOCAL * OWNED, 128), f32),
-        ],
-        0,
-    )
-    level_columns = level_rows.T
+    def level_row(b, k):
+        first = 128 * EXTRA + 3 * OWNED * b + k
+        return turned[first : first + 1, :]
+
+    level_columns = wide[pl.ds(EXTRA, DEVICES, stride=PITCH), :]
     for q in range(LOCAL * OWNED):
-        column = level_columns[:, q : q + 1]
+        lane = 3 * OWNED * (q // OWNED) + q % OWNED
+        column = level_columns[:, lane : lane + 1]
         columns[q] = jnp.broadcast_to(column, (DEVICES, 128)).astype(bf16)
 
     card_load.wait()
@@ -486,7 +502,7 @@
         level_tiles.append(
             [
                 jnp.concatenate(
-                    [jnp.broadcast_to(level_rows[OWNED * b + k : OWNED * b + k + 1], (16, 128))] * 8,
+                    [jnp.broadcast_to(level_row(b, k), (16, 128))] * 8,
                     0,
                 ).astype(bf16)
                 for k in range(OWNED)
@@ -524,7 +540,7 @@
         river_out[b, 8:9, :] = last
         total = values if b == 0 else total + values
         last_total = last if b == 0 else last_total + last
-    fold_total = (folds[82:83, :] + folds[83:84, :]) * alive_turn
+    fold_total = (folds[81:82, :] + folds[82:83, :]) * alive_turn
     for k in range(OWNED):
         lanes = slice(128 * k, 128 * k + 128)
         marks[pl.ds(k, 8, stride=OWNED), :] = total[:, lanes]
@@ -548,7 +564,7 @@
         ),
         scratch_shapes=[
             pltpu.SMEM(turn_cards.shape, jnp.int32),
-            pltpu.VMEM((DEVICES, PITCH, 128), jnp.float32),
+            pltpu.VMEM((DEVICES * PITCH, 128), jnp.float32),
             pltpu.VMEM((DEVICES * BLOCKS, 128), jnp.float32),
             pltpu.VMEM((LOCAL * BOARD_ROWS, HANDS), jnp.bfloat16),
             pltpu.VMEM((LOCAL * OWNED, DEVICES, 128), jnp.bfloat16),
@@ -607,16 +623,21 @@
         pairs[first + 52] = 0.5
 
     turn_cards = turn_cards.T
-    packed = send(
-        turn_cards, jnp.transpose(cum_turn, (0, 2, 1)), opp_init.T, strength, cum_river
+    packed, pairs = send(
+        turn_cards,
+        jnp.transpose(cum_turn, (0, 2, 1)),
+        opp_init.T,
+        strength,
+        cum_river,
+        jnp.asarray(pairs, jnp.bfloat16),
     )
-    packed = packed.reshape(DEVICES, BLOCKS, 128)
+    packed = packed.reshape(DEVICES, BLOCKS // 2, 2, 128)
     recv = lax.all_to_all(packed, AXES, split_axis=0, concat_axis=0, tiled=True)
     river, sums = boards(
         turn_cards,
         jnp.asarray(cards),
         recv.reshape(DEVICES * BLOCKS, 128),
-        jnp.asarray(pairs, jnp.bfloat16),
+        pairs,
     )
     back = lax.all_to_all(
         sums.reshape(DEVICES, 1, 128), AXES, split_axis=0, concat_axis=0, tiled=True

time: 52.3 us -> 51.3 us (0.981)
  blocking collectives: 28.1 us -> 27.4 us
    all_to_all x1, blocking collectives: 28.1 us -> 27.4 us  [body(): recv = lax.all_to_all(packed, AXES, split_axis=0, concat_axis=0, tiled=True)]
where the time goes in v4:
time: 51.3 us; the launch traced here: 51.2 us
  blocking collectives  27.4 us (53%)
  Pallas kernels  9.31 us (18%)
  waiting for transfers between devices  7.51 us (15%)
  starting transfers between devices  3.93 us (8%)
  local copies, waits for them, and re-layouts  2.36 us (5%)
  between operations  0.68 us (1%)
    all_to_all x1, blocking collectives, body(): recv = lax.all_to_all(packed, AXES, split_axis=0, concat_axis=0, tiled=True)  27.4 us
    all_to_all x1, waiting for transfers between devices, body(): lax.all_to_all(sums.reshape(DEVICES, 1, 128), AXES, split_axis=0, concat_...  7.51 us
    pallas_call x1, Pallas kernels, boards(): pl.pallas_call(board_kernel, in_specs=[hbm, vmem, vmem, vmem], out_specs=...  4.94 us
    all_to_all x1, starting transfers between devices, body(): lax.all_to_all(sums.reshape(DEVICES, 1, 128), AXES, split_axis=0, concat_...  3.93 us
    pallas_call x1, Pallas kernels, send(): pl.pallas_call(send_kernel, in_specs=[pl.BlockSpec(memory_space=pl.ANY)]...  3.67 us
    reshape x1, local copies, waits for them, and re-layouts, body(): jnp.transpose(river, (0, 1, 3, 2)).reshape(LOCAL, LINES, HANDS)  1.75 us
  transfers between devices with their start and end apart: 1, of which 1 were waited for; matrix products, arithmetic and copies ran while one was open for 5% of the time, Pallas kernels for 0%

profile of v4, /device:TPU:1, one launch (start us, length us, event | category | flops | bytes accessed | tf_op | source)
XLA Modules:
  0.0 51.2 jit_solution(2374264660553859015)
XLA Ops:
  0.6 0.0 copy-start
  0.6 3.7 %send_reach.1 = (bf16[2816,128]{1,0:T(8,128)(2,1)S(1)}, bf16[1664,1408]{1,0:T(8,128)(2,1)S(1)}) custom-call(s32[4,8]{1,0:T(4,128)} %bitcast.21, f32[11,8,13]{2,1,0:T(8,128)} %bitcast.20, f32[8,11]{1,0:T(8,128)} %bitcast.23, s32[11,384]{1,0:T(8,128)} %strength_hbm.1, f32[11,9,13,384]{3,2,1,0:T(8,128)} %cum_river.1, bf16[1664,1408]{1,0:T(8,128)(2,1)} %constant.4.clone.pairs_hbm), custom_call_target="tpu_custom_call" | custom-call | tf_op jit(solution)/shard_map/send_reach/pallas_call | solution.py:357
  4.3 27.4 %all_to_all.10 = bf16[128,11,2,128]{3,2,1,0:T(2,128)(2,1)S(1)} all-to-all(bf16[128,11,2,128]{3,2,1,0:T(2,128)(2,1)S(1)} %bitcast.17), channel_id=1, replica_groups=mesh['board'=16,'hand'=8] {'board','hand'}, dimensions={0} | all-to-all | bytes 1441792 | tf_op jit(solution)/shard_map/all_to_all | solution.py:635
  31.7 0.0 copy-done
  31.7 4.9 %board_values.1 = (f32[3,9,1408]{2,1,0:T(8,128)S(1)}, f32[128,128]{1,0:T(8,128)}) custom-call(s32[4,8]{1,0:T(4,128)} %bitcast.22, s32[8,1408]{1,0:T(8,128)S(1)} %copy-done, bf16[2816,128]{1,0:T(8,128)(2,1)S(1)} %bitcast.16, bf16[1664,1408]{1,0:T(8,128)(2,1)S(1)} %get-tuple-element.7.pairs), custom_call_target="tpu_custom_call" | custom-call | tf_op jit(solution)/shard_map/board_values/pallas_call | solution.py:557
  36.7 3.9 %all-to-all-start.1 = ((f32[128,1,128]{2,1,0:T(1,128)}), f32[128,1,128]{2,1,0:T(1,128)S(1)}, u32[]{:S(2)}, u32[]{:S(2)}) async-start(f32[128,1,128]{2,1,0:T(1,128)} %bitcast.8), calls=%async_computation.1 | async-start | bytes 131072 | tf_op jit(solution)/shard_map/all_to_all | solution.py:642
  40.6 0.6 %copy.13 = f32[3,9,128,11]{3,2,0,1:T(8,128)S(1)} copy(f32[3,9,128,11]{2,3,1,0:T(8,128)S(1)} %bitcast.19) | data formatting | bytes 304128 | tf_op jit(solution)/shard_map/transpose | solution.py:646
  41.2 1.7 %reshape.25 = f32[3,9,1408]{2,0,1:T(4,128)} reshape(f32[3,9,128,11]{3,2,0,1:T(8,128)S(1)} %copy.13) | data formatting | bytes 304128 | tf_op jit(solution)/shard_map/reshape | solution.py:646
  43.0 7.5 %all-to-all-done.1 = f32[128,1,128]{2,1,0:T(1,128)S(1)} async-done(((f32[128,1,128]{2,1,0:T(1,128)}), f32[128,1,128]{2,1,0:T(1,128)S(1)}, u32[]{:S(2)}, u32[]{:S(2)}) %all-to-all-start.1) | async-done | bytes 65568 | tf_op jit(solution)/shard_map/all_to_all | solution.py:642
  50.5 0.7 %turn_values.1 = f32[8,11]{1,0:T(8,128)} custom-call(f32[128,128]{1,0:T(8,128)S(1)} %bitcast.18), custom_call_target="tpu_custom_call" | custom-call | tf_op jit(solution)/shard_map/turn_values/pallas_call | solution.py:601
  (1 shorter events, 0.0 us)
Async XLA Ops:
  0.6 31.1 %copy-start = (s32[8,1408]{1,0:T(8,128)S(1)}, s32[8,1408]{1,0:T(8,128)}, u32[]{:S(2)}) copy-start(s32[8,1408]{1,0:T(8,128)} %constant.5.clone.cards) | copy-start | bytes 135172
  36.7 13.8 %all-to-all-start.1 = ((f32[128,1,128]{2,1,0:T(1,128)}), f32[128,1,128]{2,1,0:T(1,128)S(1)}, u32[]{:S(2)}, u32[]{:S(2)}) async-start(f32[128,1,128]{2,1,0:T(1,128)} %bitcast.8), calls=%async_computation.1 | async-start | bytes 131072 | tf_op jit(solution)/shard_map/all_to_all | solution.py:642

commit v5 on v4

--- a/solution.py
+++ b/solution.py
@@ -11,7 +11,7 @@
 BETS = 4
 PRE_POT = 2.0
 UNROLL = True
-GROUP = 3
+GROUP = 6
 AXES = ("board", "hand")
 
 HANDS = 1408

time: 51.3 us -> 51.2 us (level)
  no operation moved by 1% of the time
where the time goes in v5:
time: 51.2 us; the launch traced here: 51 us
  blocking collectives  27.4 us (54%)
  Pallas kernels  9.17 us (18%)
  waiting for transfers between devices  7.51 us (15%)
  starting transfers between devices  3.93 us (8%)
  local copies, waits for them, and re-layouts  2.36 us (5%)
  between operations  0.68 us (1%)
    all_to_all x1, blocking collectives, body(): recv = lax.all_to_all(packed, AXES, split_axis=0, concat_axis=0, tiled=True)  27.4 us
    all_to_all x1, waiting for transfers between devices, body(): lax.all_to_all(sums.reshape(DEVICES, 1, 128), AXES, split_axis=0, concat_...  7.51 us
    pallas_call x1, Pallas kernels, boards(): pl.pallas_call(board_kernel, in_specs=[hbm, vmem, vmem, vmem], out_specs=...  4.94 us
    all_to_all x1, starting transfers between devices, body(): lax.all_to_all(sums.reshape(DEVICES, 1, 128), AXES, split_axis=0, concat_...  3.93 us
    pallas_call x1, Pallas kernels, send(): pl.pallas_call(send_kernel, in_specs=[pl.BlockSpec(memory_space=pl.ANY)]...  3.53 us
    reshape x1, local copies, waits for them, and re-layouts, body(): jnp.transpose(river, (0, 1, 3, 2)).reshape(LOCAL, LINES, HANDS)  1.75 us
  transfers between devices with their start and end apart: 1, of which 1 were waited for; matrix products, arithmetic and copies ran while one was open for 5% of the time, Pallas kernels for 0%

profile of v5, /device:TPU:1, one launch (start us, length us, event | category | flops | bytes accessed | tf_op | source)
XLA Modules:
  0.0 51.0 jit_solution(9077231479858480980)
XLA Ops:
  0.6 0.0 copy-start
  0.6 3.5 %send_reach.1 = (bf16[2816,128]{1,0:T(8,128)(2,1)S(1)}, bf16[1664,1408]{1,0:T(8,128)(2,1)S(1)}) custom-call(s32[4,8]{1,0:T(4,128)} %bitcast.21, f32[11,8,13]{2,1,0:T(8,128)} %bitcast.20, f32[8,11]{1,0:T(8,128)} %bitcast.23, s32[11,384]{1,0:T(8,128)} %strength_hbm.1, f32[11,9,13,384]{3,2,1,0:T(8,128)} %cum_river.1, bf16[1664,1408]{1,0:T(8,128)(2,1)} %constant.4.clone.pairs_hbm), custom_call_target="tpu_custom_call" | custom-call | tf_op jit(solution)/shard_map/send_reach/pallas_call | solution.py:357
  4.2 27.4 %all_to_all.10 = bf16[128,11,2,128]{3,2,1,0:T(2,128)(2,1)S(1)} all-to-all(bf16[128,11,2,128]{3,2,1,0:T(2,128)(2,1)S(1)} %bitcast.17), channel_id=1, replica_groups=mesh['board'=16,'hand'=8] {'board','hand'}, dimensions={0} | all-to-all | bytes 1441792 | tf_op jit(solution)/shard_map/all_to_all | solution.py:635
  31.6 0.0 copy-done
  31.6 4.9 %board_values.1 = (f32[3,9,1408]{2,1,0:T(8,128)S(1)}, f32[128,128]{1,0:T(8,128)}) custom-call(s32[4,8]{1,0:T(4,128)} %bitcast.22, s32[8,1408]{1,0:T(8,128)S(1)} %copy-done, bf16[2816,128]{1,0:T(8,128)(2,1)S(1)} %bitcast.16, bf16[1664,1408]{1,0:T(8,128)(2,1)S(1)} %get-tuple-element.7.pairs), custom_call_target="tpu_custom_call" | custom-call | tf_op jit(solution)/shard_map/board_values/pallas_call | solution.py:557
  36.5 3.9 %all-to-all-start.1 = ((f32[128,1,128]{2,1,0:T(1,128)}), f32[128,1,128]{2,1,0:T(1,128)S(1)}, u32[]{:S(2)}, u32[]{:S(2)}) async-start(f32[128,1,128]{2,1,0:T(1,128)} %bitcast.8), calls=%async_computation.1 | async-start | bytes 131072 | tf_op jit(solution)/shard_map/all_to_all | solution.py:642
  40.5 0.6 %copy.13 = f32[3,9,128,11]{3,2,0,1:T(8,128)S(1)} copy(f32[3,9,128,11]{2,3,1,0:T(8,128)S(1)} %bitcast.19) | data formatting | bytes 304128 | tf_op jit(solution)/shard_map/transpose | solution.py:646
  41.1 1.7 %reshape.25 = f32[3,9,1408]{2,0,1:T(4,128)} reshape(f32[3,9,128,11]{3,2,0,1:T(8,128)S(1)} %copy.13) | data formatting | bytes 304128 | tf_op jit(solution)/shard_map/reshape | solution.py:646
  42.8 7.5 %all-to-all-done.1 = f32[128,1,128]{2,1,0:T(1,128)S(1)} async-done(((f32[128,1,128]{2,1,0:T(1,128)}), f32[128,1,128]{2,1,0:T(1,128)S(1)}, u32[]{:S(2)}, u32[]{:S(2)}) %all-to-all-start.1) | async-done | bytes 65568 | tf_op jit(solution)/shard_map/all_to_all | solution.py:642
  50.3 0.7 %turn_values.1 = f32[8,11]{1,0:T(8,128)} custom-call(f32[128,128]{1,0:T(8,128)S(1)} %bitcast.18), custom_call_target="tpu_custom_call" | custom-call | tf_op jit(solution)/shard_map/turn_values/pallas_call | solution.py:601
  (1 shorter events, 0.0 us)
Async XLA Ops:
  0.6 30.9 %copy-start = (s32[8,1408]{1,0:T(8,128)S(1)}, s32[8,1408]{1,0:T(8,128)}, u32[]{:S(2)}) copy-start(s32[8,1408]{1,0:T(8,128)} %constant.5.clone.cards) | copy-start | bytes 135172
  36.5 13.8 %all-to-all-start.1 = ((f32[128,1,128]{2,1,0:T(1,128)}), f32[128,1,128]{2,1,0:T(1,128)S(1)}, u32[]{:S(2)}, u32[]{:S(2)}) async-start(f32[128,1,128]{2,1,0:T(1,128)} %bitcast.8), calls=%async_computation.1 | async-start | bytes 131072 | tf_op jit(solution)/shard_map/all_to_all | solution.py:642
